TPU v7x, 32 devices: a whole 2x2x4 slice. The times are simulated.
32 devices in a mesh: elem: 8 (over y, x, core), face: 4 (over z).
Axes of the slice: x: 2, y: 2, z: 4, core: 2. Of those that a mesh axis runs over, the one named last changes fastest.
Arguments:
- state: float32 [10, 72, 16384], P(None, None, ('elem', 'face')), may hold values from -6 to 6
- metric: float32 [16, 1024], P(None, ('elem', 'face')), may hold values from 0.5 to 2
- neighbours: int32 [4, 1024], P(None, ('elem', 'face')), may hold values from 0 to 1023, as said below
- cost_class: int32 [16, 1024], P(None, ('elem', 'face')), may hold values from 1 to 4
- batch_slot: int32 [16, 1024], replicated, may hold values from 0 to 16383, as said below
- level_mix: float32 [10, 72, 72], replicated, may hold values from -0.75 to 0.75
- field_coupling_matrix: float32 [10, 10], replicated, may hold values from -2 to 2
Outputs:
- state_out: float32 [10, 72, 16384], P(None, None, ('elem', 'face'))
- physics_state: float32 [10, 72, 16384], P(None, None, ('elem', 'face'))
Inputs may be any that keep to these rules, and one draw needn't show every extreme that they name: Blocks are the element ranges [b * 32, (b + 1) * 32), in the order of the devices. The elements form a closed grid of rows of 8 elements, 4 rows a block; neighbours[0], [1], [2], [3] name the elements east, west, north and south, which are mutual (the west neighbour of the east one is the element itself, likewise north and south, and east of north is north of east). East and west neighbours lie in the element's own block; a north neighbour lies in the same block or in the next one, a south neighbour in the same block or the previous one, cyclically over the blocks; in each block exactly 8 elements have their north neighbour in the next block and 8 their south neighbour in the previous one. `batch_slot`: A permutation of the columns; batch c holds the places [c * 512, (c + 1) * 512). Every batch holds exactly 16 columns of every block, and within a batch cost_class never rises from one place to the next.
All inputs are finite; a program needn't handle non-finite values.
Results may differ from a plain program's by a relative error of at most 0.0001.
Values sent between devices are 32-bit elements; how exact they have to be, the bound alone decides.
A program may use at most 128 MiB of HBM per device.

v0:
```python
from functools import partial
import math

import jax
import jax.numpy as jnp
import numpy as np
from jax import lax
from jax.sharding import PartitionSpec as P

ROWS_DEV = 4
SUBSTEPS = 3
SWEEPS = 4


PHYSICS_RATE = 0.1
TIME_STEP = 0.02


def from_behind(array, axis, by):
    length = lax.axis_size(axis)
    return lax.ppermute(array, axis, [(i, (i + by) % length) for i in range(length)])


def gll_matrices():
    gll_nodes = np.array([-1.0, -1.0 / np.sqrt(5.0), 1.0 / np.sqrt(5.0), 1.0])
    derivative = np.zeros((4, 4))
    for target in range(4):
        for source in range(4):
            if target == source:
                derivative[target, source] = sum(
                    (
                        1.0 / (gll_nodes[source] - gll_nodes[middle])
                        for middle in range(4)
                        if middle != source
                    )
                )
            else:
                numerator = np.prod(
                    [
                        gll_nodes[target] - gll_nodes[middle]
                        for middle in range(4)
                        if middle != source and middle != target
                    ]
                )
                denominator = np.prod(
                    [
                        gll_nodes[source] - gll_nodes[middle]
                        for middle in range(4)
                        if middle != source
                    ]
                )
                derivative[target, source] = numerator / denominator
    across = np.kron(np.eye(4), derivative).astype(np.float32)
    upward = np.kron(derivative, np.eye(4)).astype(np.float32)
    return (jnp.asarray(across), jnp.asarray(upward))


def invert(permutation):
    extent = permutation.shape[0]
    return jnp.zeros((extent,), jnp.int32).at[permutation].set(jnp.arange(extent, dtype=jnp.int32))


def advect(current, across, upward):
    along_x = jnp.einsum("pq,...qe->...pe", across, current, precision=lax.Precision.HIGHEST)
    along_y = jnp.einsum("pq,...qe->...pe", upward, current, precision=lax.Precision.HIGHEST)
    return -(current[0:1] * along_x + current[1:2] * along_y)


def rank_of(targets, remote):
    smaller = (targets[None, :] < targets[:, None]) & remote[None, :]
    return jnp.sum(smaller.astype(jnp.int32), axis=1)


def cross_rows(south_row, north_row, neighbours, myself):
    members = south_row.shape[-1]
    boundary = members // ROWS_DEV
    sequence = jnp.arange(members, dtype=jnp.int32)
    remote_up = neighbours[2] // members != myself
    remote_down = neighbours[3] // members != myself
    up_list = jnp.argsort(jnp.where(remote_up, sequence, sequence + members))[:boundary]
    down_list = jnp.argsort(jnp.where(remote_down, sequence, sequence + members))[:boundary]
    from_prev = from_behind(jnp.take(north_row, up_list, axis=-1), ("elem", "face"), 1)
    from_next = from_behind(jnp.take(south_row, down_list, axis=-1), ("elem", "face"), -1)
    up_rank = jnp.where(remote_up, rank_of(neighbours[2], remote_up), 0)
    down_rank = jnp.where(remote_down, rank_of(neighbours[3], remote_down), 0)
    local_up = jnp.where(remote_up, 0, neighbours[2] - myself * members)
    local_down = jnp.where(remote_down, 0, neighbours[3] - myself * members)
    north_side = jnp.where(
        remote_up, jnp.take(from_next, up_rank, axis=-1), jnp.take(south_row, local_up, axis=-1)
    )
    south_side = jnp.where(
        remote_down,
        jnp.take(from_prev, down_rank, axis=-1),
        jnp.take(north_row, local_down, axis=-1),
    )
    return (north_side, south_side)


def combine(values, neighbours, myself):
    leading = values.shape[:-2]
    members = values.shape[-1]
    layout = values.reshape(leading + (4, 4, members))
    west_edge = layout[..., :, 0, :]
    east_edge = layout[..., :, 3, :]
    base_id = myself * members
    new_east = east_edge + jnp.take(west_edge, neighbours[0] - base_id, axis=-1)
    new_west = west_edge + jnp.take(east_edge, neighbours[1] - base_id, axis=-1)
    stepped = jnp.stack([new_west, layout[..., :, 1, :], layout[..., :, 2, :], new_east], axis=-2)
    south_row = stepped[..., 0, :, :]
    north_row = stepped[..., 3, :, :]
    north_side, south_side = cross_rows(south_row, north_row, neighbours, myself)
    physics_output = jnp.stack(
        [
            south_row + south_side,
            stepped[..., 1, :, :],
            stepped[..., 2, :, :],
            north_row + north_side,
        ],
        axis=-3,
    )
    return physics_output.reshape(values.shape)


def relax(segment, active, level_mix, field_coupling_matrix):
    level_blended = jnp.einsum("flm,fmc->flc", level_mix, segment, precision=lax.Precision.HIGHEST)
    field_coupled = jnp.einsum(
        "mx,xaq->maq", field_coupling_matrix, level_blended, precision=lax.Precision.HIGHEST
    )
    return jnp.where(
        active[None, None, :], segment + PHYSICS_RATE * jnp.tanh(field_coupled), segment
    )


def advance_block(
    threshold, block_cols, weighted, level_mix, field_coupling_matrix, block_index, current
):
    offset_cols = block_index * block_cols
    segment = lax.dynamic_slice_in_dim(current, offset_cols, block_cols, axis=2)
    active = lax.dynamic_slice_in_dim(weighted, offset_cols, block_cols) > threshold
    return lax.dynamic_update_slice_in_dim(
        current, relax(segment, active, level_mix, field_coupling_matrix), offset_cols, axis=2
    )


def advance_sorted(columns, classes, level_mix, field_coupling_matrix):
    width = columns.shape[-1]
    block_cols = math.gcd(width, 256)
    weighted = classes * SWEEPS

    def physics_pass(threshold, current):
        live_count = jnp.sum((weighted > threshold).astype(jnp.int32))
        trip_count = (live_count + block_cols - 1) // block_cols
        return lax.fori_loop(
            0,
            trip_count,
            partial(
                advance_block, threshold, block_cols, weighted, level_mix, field_coupling_matrix
            ),
            current,
        )

    return lax.fori_loop(0, 4 * SWEEPS, physics_pass, columns)


def per_device(state, metric, neighbours, cost_class, batch_slot, level_mix, field_coupling_matrix):
    fields, levels, columns_dev = state.shape
    points, members = metric.shape
    grid_state = jnp.transpose(state.reshape(fields, levels, members, points), (0, 1, 3, 2))
    devices = lax.axis_size(("elem", "face"))
    myself = lax.axis_index(("elem", "face"))
    sequence = jnp.arange(columns_dev, dtype=jnp.int32)
    columns = grid_state.reshape(fields, levels, columns_dev)
    own_class = cost_class.reshape(columns_dev)
    my_slots = lax.dynamic_slice_in_dim(batch_slot, myself * members, members, axis=1).reshape(
        columns_dev
    )
    send_order = jnp.argsort(my_slots)
    send_back = invert(send_order)
    column_of = invert(batch_slot.reshape(batch_slot.size))
    owned = lax.dynamic_slice_in_dim(column_of, myself * columns_dev, columns_dev)
    source = owned % (members * devices) // members
    arrival = jnp.argsort(source * columns_dev + sequence)
    arrival_back = invert(arrival)
    outgoing = jnp.take(columns, send_order, axis=2).reshape(fields * levels, columns_dev)
    class_row = jnp.take(own_class, send_order).astype(jnp.float32)[None, :]
    arrived, arrived_class = (
        lax.all_to_all(outgoing, ("elem", "face"), split_axis=1, concat_axis=1, tiled=True),
        lax.all_to_all(class_row, ("elem", "face"), split_axis=1, concat_axis=1, tiled=True),
    )
    batch_cols = jnp.take(arrived, arrival_back, axis=1).reshape(fields, levels, columns_dev)
    batch_class = jnp.take(arrived_class[0], arrival_back).astype(jnp.int32)
    physics_state = advance_sorted(batch_cols, batch_class, level_mix, field_coupling_matrix)
    change = jnp.take(
        (physics_state - batch_cols).reshape(fields * levels, columns_dev), arrival, axis=1
    )
    returned = lax.all_to_all(change, ("elem", "face"), split_axis=1, concat_axis=1, tiled=True)
    physics_tendency = jnp.take(returned, send_back, axis=1)
    physics_tendency = physics_tendency.reshape(grid_state.shape)
    across, upward = gll_matrices()
    mass_total = combine(metric[None, None], neighbours, myself)
    current = grid_state
    for advection_substep in range(SUBSTEPS):
        rate = advect(current, across, upward)
        updated = current + TIME_STEP * rate + physics_tendency / SUBSTEPS
        current = combine(metric * updated, neighbours, myself) / mass_total
    state_out = jnp.transpose(current, (0, 1, 3, 2)).reshape(fields, levels, columns_dev)
    return (state_out, physics_state)


def solution(mesh):
    placed = (
        P(None, None, ("elem", "face")),
        P(None, ("elem", "face")),
        P(None, ("elem", "face")),
        P(None, ("elem", "face")),
        P(),
        P(),
        P(),
    )
    return jax.shard_map(
        per_device,
        mesh=mesh,
        in_specs=placed,
        out_specs=(P(None, None, ("elem", "face")), P(None, None, ("elem", "face"))),
        check_vma=False,
    )
```

profile of v0, /device:TPU:0, one launch (start us, length us, event | category | flops | bytes accessed | tf_op | source)
XLA Modules:
  0.0 420.9 jit_solution(4685387157153293738)
XLA Ops:
  2.3 3.8 sort.74
  6.0 3.5 gather_fusion.1
  10.2 7.3 %all-to-all-start.1 = ((f32[1,32,16]{2,0,1:T(1,128)}), f32[1,32,16]{2,0,1:T(1,128)S(1)}, u32[]{:S(2)}, u32[]{:S(2)}) async-start(f32[1,32,16]{2,0,1:T(1,128)} %bitcast.20), calls=%async_computation.1 | async-start | bytes 32768 | tf_op jit(solution)/shard_map/all_to_all | solution.py:188
  22.9 3.5 copy.239
  26.5 5.2 %gather_fusion = f32[512,10,72]{2,1,0:T(8,128)} fusion(f32[10,72,512]{1,0,2:T(8,128)} %copy.239, s32[1024]{0:T(1024)S(1)} %pad_clamp_fusion.11), kind=kCustom, calls=%fused_computation.35 | custom fusion | bytes 2951168 | tf_op jit(solution)/shard_map/jit(_take)/gather | solution.py:184
  31.7 3.5 gather.36
  36.5 5.8 %all-to-all-start = ((f32[720,32,16]{0,2,1:T(8,128)}), f32[720,32,16]{0,2,1:T(8,128)S(1)}, u32[]{:S(2)}, u32[]{:S(2)}) async-start(f32[720,32,16]{0,2,1:T(8,128)} %broadcast_select_fusion.1), calls=%async_computation | async-start | bytes 3145728 | tf_op jit(solution)/shard_map/all_to_all | solution.py:187
  46.7 60.3 %scatter_custom_fusion = s32[16384]{0:T(1024)S(1)} fusion(s32[16384]{0:T(1024)S(1)} %bitcast.431, s32[16384]{0:T(1024)S(1)} %iota.45, s32[]{:T(128)} %constant.280.clone.1), kind=kCustom, calls=%fused_computation.154 | custom fusion | bytes 65540 | tf_op jit(solution)/shard_map/scatter | solution.py:60
  107.2 3.8 sort.75
  115.0 3.5 gather_fusion.2
  123.8 80.3 %while.53 = (s32[]{:T(128)}, f32[10,72,512]{2,1,0:T(8,128)S(1)}, s32[512]{0:T(512)S(1)}, f32[10,72,72]{2,1,0:T(8,128)S(1)}, f32[10,10]{1,0:T(8,128)S(1)}, /*inde...) while((s32[]{:T(128)}, f32[10,72,512]{2,1,0:T(8,128)S(1)}, ...), condition=%wide.region_8.10_spmd, body=%wide.region_4.9_spmd.sunk | while | flops 181925648 | bytes 5976802 | solution.py:162
  125.2 5.7 %while.54 = (s32[]{:T(128)}, f32[10,72,512]{2,1,0:T(8,128)S(1)}, s32[]{:T(128)}, s32[512]{0:T(512)S(1)}, s32[]{:T(128)}, /*index=5*/f32[10,72,72]{2,1,0:T(8,128)...) while((s32[]{:T(128)}, f32[10,72,512]{2,1,0:T(8,128)S(1)}, s32[]{:T(128)}, ...), condition=%wide.region_7.8_spmd, body=%wide.region_6.7_spmd.sunk | while | flops 181924096 | bytes 5974331 | solution.py:153
  132.4 5.7 %while.54 = (s32[]{:T(128)}, f32[10,72,512]{2,1,0:T(8,128)S(1)}, s32[]{:T(128)}, s32[512]{0:T(512)S(1)}, s32[]{:T(128)}, /*index=5*/f32[10,72,72]{2,1,0:T(8,128)...) while((s32[]{:T(128)}, f32[10,72,512]{2,1,0:T(8,128)S(1)}, s32[]{:T(128)}, ...), condition=%wide.region_7.8_spmd, body=%wide.region_6.7_spmd.sunk | while | flops 181924096 | bytes 5974331 | solution.py:153
  139.6 5.7 %while.54 = (s32[]{:T(128)}, f32[10,72,512]{2,1,0:T(8,128)S(1)}, s32[]{:T(128)}, s32[512]{0:T(512)S(1)}, s32[]{:T(128)}, /*index=5*/f32[10,72,72]{2,1,0:T(8,128)...) while((s32[]{:T(128)}, f32[10,72,512]{2,1,0:T(8,128)S(1)}, s32[]{:T(128)}, ...), condition=%wide.region_7.8_spmd, body=%wide.region_6.7_spmd.sunk | while | flops 181924096 | bytes 5974331 | solution.py:153
  146.7 5.7 %while.54 = (s32[]{:T(128)}, f32[10,72,512]{2,1,0:T(8,128)S(1)}, s32[]{:T(128)}, s32[512]{0:T(512)S(1)}, s32[]{:T(128)}, /*index=5*/f32[10,72,72]{2,1,0:T(8,128)...) while((s32[]{:T(128)}, f32[10,72,512]{2,1,0:T(8,128)S(1)}, s32[]{:T(128)}, ...), condition=%wide.region_7.8_spmd, body=%wide.region_6.7_spmd.sunk | while | flops 181924096 | bytes 5974331 | solution.py:153
  213.1 5.8 %all-to-all-start.2 = ((f32[720,32,16]{0,2,1:T(8,128)}), f32[720,32,16]{0,2,1:T(8,128)S(1)}, u32[]{:S(2)}, u32[]{:S(2)}) async-start(f32[720,32,16]{0,2,1:T(8,128)} %bitcast.23), calls=%async_computation.2 | async-start | bytes 3145728 | tf_op jit(solution)/shard_map/all_to_all | solution.py:196
  228.0 5.5 %fusion.84 = f32[16,10,72,32]{2,0,3,1:T(8,128)} fusion(f32[16,16,1,1]{1,0,3,2:T(8,128)S(1)} %copy-done.28, f32[10,72,16,32]{1,2,3,0:T(8,128)} %bitcast.398), kind=kOutput, calls=%fused_computation.268 | convolution fusion | flops 70778880 | bytes 2950144 | tf_op jit(solution)/shard_map/pq,...qe->...pe/dot_general | solution.py:64
  233.6 16.7 %collective-permute-done.2 = f32[1,1,4,8]{3,2,1,0:T(4,128)S(1)} collective-permute-done((f32[1,1,4,8]{3,2,1,0:T(4,128)S(1)}, f32[1,1,4,8]{3,2,1,0:T(4,128)S(1)}, u32[]{:S(2)}, u32[]{:S(2)}) %collective-permute-start.2) | collective-permute-done | bytes 160 | tf_op jit(solution)/shard_map/ppermute | solution.py:21
  254.1 5.7 %collective-permute-done.3 = f32[1,1,4,8]{3,2,1,0:T(4,128)S(1)} collective-permute-done((f32[1,1,4,8]{3,2,1,0:T(4,128)S(1)}, f32[1,1,4,8]{3,2,1,0:T(4,128)S(1)}, u32[]{:S(2)}, u32[]{:S(2)}) %collective-permute-start.3) | collective-permute-done | bytes 160 | tf_op jit(solution)/shard_map/ppermute | solution.py:21
  264.5 4.9 %div.102 = f32[10,72,16,32]{1,0,3,2:T(8,128)} reshape(f32[720,512]{0,1:T(8,128)} %bitcast_multiply_fusion.6) | data formatting | bytes 2949120 | tf_op jit(solution)/shard_map/div | solution.py:204
  269.4 7.1 %fusion.30 = f32[10,72,16,32]{1,2,3,0:T(8,128)S(1)} fusion(f32[10,72,16,32]{1,2,3,0:T(8,128)S(1)} %bitcast.399, f32[16,10,72,32]{2,0,3,1:T(8,128)} %fusion.84, f32[16,16,1,1]{1,0,3,2:T(8,128)S(1)} %copy-done.27, f32[72,16,32]{0,1,2:T(8,128)S(1)} %copy-done.26, f32[72,16,32]{0,1,2:T(8,128)S(1)} %get-tuple-element.339, f32[16,32]{0,1:T(8,128)S(1)} %copy.236, ...), kind=kOutput, calls=%fused_computation.89 | convolution fusion | flops 73728000 | bytes 6196224 | tf_op jit(solution)/shard_map/pq,...qe->...pe/dot_general | solution.py:65
  295.0 4.7 %collective-permute-done = f32[10,72,4,8]{1,2,0,3:T(4,128)S(1)} collective-permute-done((f32[10,72,4,8]{1,2,0,3:T(4,128)}, f32[10,72,4,8]{1,2,0,3:T(4,128)S(1)}, u32[]{:S(2)}, u32[]{:S(2)}) %collective-permute-start) | collective-permute-done | bytes 92192 | tf_op jit(solution)/shard_map/ppermute | solution.py:21
  301.6 3.3 fusion.51
  310.3 2.9 gather_fusion.13
  323.0 4.3 %fusion.24 = f32[10,72,16,32]{1,2,3,0:T(8,128)S(1)} fusion(f32[10,72,16,32]{1,2,3,0:T(8,128)S(1)} %broadcast_divide_fusion.2, f32[10,72,32,16]{1,3,2,0:T(8,128)S(1)} %fusion.85, f32[16,16,1,1]{1,0,3,2:T(8,128)S(1)} %copy-done.27, f32[72,16,32]{0,1,2:T(8,128)S(1)} %get-tuple-element.336, f32[72,16,32]{0,1,2:T(8,128)S(1)} %get-tuple-element.335, ...), kind=kOutput, calls=%fused_computation.81 | convolution fusion | flops 73728000 | bytes 6196224 | tf_op jit(solution)/shard_map/pq,...qe->...pe/dot_general | solution.py:65
  331.2 3.0 gather_fusion.22
  344.4 5.6 %collective-permute-done.4 = f32[10,72,4,8]{1,2,0,3:T(4,128)S(1)} collective-permute-done((f32[10,72,4,8]{1,2,0,3:T(4,128)}, f32[10,72,4,8]{1,2,0,3:T(4,128)S(1)}, u32[]{:S(2)}, u32[]{:S(2)}) %collective-permute-start.4) | collective-permute-done | bytes 92192 | tf_op jit(solution)/shard_map/ppermute | solution.py:21
  351.8 3.4 fusion.46
  371.9 4.3 %fusion.18 = f32[10,72,16,32]{1,2,3,0:T(8,128)S(1)} fusion(f32[10,72,16,32]{1,2,3,0:T(8,128)S(1)} %broadcast_divide_fusion.1, f32[10,72,32,16]{1,3,2,0:T(8,128)S(1)} %fusion.86, f32[16,16,1,1]{1,0,3,2:T(8,128)S(1)} %copy-done.27, f32[72,16,32]{0,1,2:T(8,128)S(1)} %get-tuple-element.332, f32[72,16,32]{0,1,2:T(8,128)S(1)} %get-tuple-element.331, ...), kind=kOutput, calls=%fused_computation.73 | convolution fusion | flops 73728000 | bytes 6196224 | tf_op jit(solution)/shard_map/pq,...qe->...pe/dot_general | solution.py:65
  380.1 3.0 gather_fusion.30
  392.4 6.8 %collective-permute-done.6 = f32[10,72,4,8]{1,2,0,3:T(4,128)S(1)} collective-permute-done((f32[10,72,4,8]{1,2,0,3:T(4,128)}, f32[10,72,4,8]{1,2,0,3:T(4,128)S(1)}, u32[]{:S(2)}, u32[]{:S(2)}) %collective-permute-start.6) | collective-permute-done | bytes 92192 | tf_op jit(solution)/shard_map/ppermute | solution.py:21
  401.1 3.3 fusion.41
  (365 shorter events, 250.0 us)
Async XLA Ops:
  10.2 26.3 %all-to-all-start.1 = ((f32[1,32,16]{2,0,1:T(1,128)}), f32[1,32,16]{2,0,1:T(1,128)S(1)}, u32[]{:S(2)}, u32[]{:S(2)}) async-start(f32[1,32,16]{2,0,1:T(1,128)} %bitcast.20), calls=%async_computation.1 | async-start | bytes 32768 | tf_op jit(solution)/shard_map/all_to_all | solution.py:188
  35.1 7.3 %copy-start.29 = (f32[16,32]{1,0:T(8,128)S(1)}, f32[16,32]{1,0:T(8,128)}, u32[]{:S(2)}) copy-start(f32[16,32]{1,0:T(8,128)} %param.28) | copy-start | bytes 6148
  36.5 81.9 %all-to-all-start = ((f32[720,32,16]{0,2,1:T(8,128)}), f32[720,32,16]{0,2,1:T(8,128)S(1)}, u32[]{:S(2)}, u32[]{:S(2)}) async-start(f32[720,32,16]{0,2,1:T(8,128)} %broadcast_select_fusion.1), calls=%async_computation | async-start | bytes 3145728 | tf_op jit(solution)/shard_map/all_to_all | solution.py:187
  46.1 172.8 %copy-start.33 = (pred[8]{0:T(512)(128)(4,1)}, pred[8]{0:T(512)(128)(4,1)S(1)}, u32[]{:S(2)}) copy-start(pred[8]{0:T(512)(128)(4,1)S(1)} %get-tuple-element.311) | copy-start | bytes 28
  121.7 2.0 copy-start.1
  121.7 2.0 copy-start.22
  204.1 3.4 copy-start
  213.1 14.9 %copy-start.28 = (f32[16,16,1,1]{1,0,3,2:T(8,128)S(1)}, f32[16,16,1,1]{1,0,3,2:T(8,128)}, u32[]{:S(2)}) copy-start(f32[16,16,1,1]{1,0,3,2:T(8,128)} %constant.300) | copy-start | bytes 3076
  213.1 48.1 %all-to-all-start.2 = ((f32[720,32,16]{0,2,1:T(8,128)}), f32[720,32,16]{0,2,1:T(8,128)S(1)}, u32[]{:S(2)}, u32[]{:S(2)}) async-start(f32[720,32,16]{0,2,1:T(8,128)} %bitcast.23), calls=%async_computation.2 | async-start | bytes 3145728 | tf_op jit(solution)/shard_map/all_to_all | solution.py:196
  218.9 31.4 %collective-permute-start.2 = (f32[1,1,4,8]{3,2,1,0:T(4,128)S(1)}, f32[1,1,4,8]{3,2,1,0:T(4,128)S(1)}, u32[]{:S(2)}, u32[]{:S(2)}) collective-permute-start(f32[1,1,4,8]{3,2,1,0:T(4,128)S(1)} %bitcast_select_fusion.11), channel_id=1, source_target_pairs={{0,1},{1,2},{2,3},{3,4},{4,5},{5,6},{6,7},{7,8},{8,9},{9,10},{10,1... | collective-permute-start | bytes 392 | tf_op jit(solution)/shard_map/ppermute | solution.py:21
  225.5 27.4 %copy-start.36 = (pred[8]{0:T(512)(128)(4,1)}, pred[8]{0:T(512)(128)(4,1)S(1)}, u32[]{:S(2)}) copy-start(pred[8]{0:T(512)(128)(4,1)S(1)} %get-tuple-element.319) | copy-start | bytes 28
  225.5 79.4 %copy-start.31 = (s32[1024]{0:T(1024)}, s32[1024]{0:T(1024)S(1)}, u32[]{:S(2)}) copy-start(s32[1024]{0:T(1024)S(1)} %pad_clamp_fusion.2) | copy-start | bytes 12292
  225.6 24.8 %copy-start.32 = (s32[1024]{0:T(1024)}, s32[1024]{0:T(1024)S(1)}, u32[]{:S(2)}) copy-start(s32[1024]{0:T(1024)S(1)} %pad_clamp_fusion.4) | copy-start | bytes 12292
  252.9 6.9 %collective-permute-start.3 = (f32[1,1,4,8]{3,2,1,0:T(4,128)S(1)}, f32[1,1,4,8]{3,2,1,0:T(4,128)S(1)}, u32[]{:S(2)}, u32[]{:S(2)}) collective-permute-start(f32[1,1,4,8]{3,2,1,0:T(4,128)S(1)} %bitcast_select_fusion.8), channel_id=1, source_target_pairs={{0,31},{1,0},{2,1},{3,2},{4,3},{5,4},{6,5},{7,6},{8,7},{9,8},{10,9... | collective-permute-start | bytes 392 | tf_op jit(solution)/shard_map/ppermute | solution.py:21
  261.1 1.9 copy-start.39
  264.5 4.9 %copy-start.3 = (f32[10,72,512]{1,2,0:T(8,128)S(1)}, f32[10,72,512]{1,2,0:T(8,128)}, u32[]{:S(2)}) copy-start(f32[10,72,512]{1,2,0:T(8,128)} %copy-done.2) | copy-start | bytes 4423684
  264.5 4.9 %copy-start.26 = (f32[72,16,32]{0,1,2:T(8,128)S(1)}, f32[72,16,32]{0,1,2:T(8,128)}, u32[]{:S(2)}) copy-start(f32[72,16,32]{0,1,2:T(8,128)} %get-tuple-element.340) | copy-start | bytes 442372
  264.5 4.9 %copy-start.27 = (f32[16,16,1,1]{1,0,3,2:T(8,128)S(1)}, f32[16,16,1,1]{1,0,3,2:T(8,128)}, u32[]{:S(2)}) copy-start(f32[16,16,1,1]{1,0,3,2:T(8,128)} %constant.301) | copy-start | bytes 3076
  279.4 1.9 copy-start.21
  283.0 4.4 %copy-start.7 = (f32[10,72,16,32]{1,2,3,0:T(8,128)S(1)}, f32[10,72,16,32]{1,2,3,0:T(8,128)}, u32[]{:S(2)}) copy-start(f32[10,72,16,32]{1,2,3,0:T(8,128)} %copy-done.6) | copy-start | bytes 4423684
  289.5 10.1 %collective-permute-start = (f32[10,72,4,8]{1,2,0,3:T(4,128)}, f32[10,72,4,8]{1,2,0,3:T(4,128)S(1)}, u32[]{:S(2)}, u32[]{:S(2)}) collective-permute-start(f32[10,72,4,8]{1,2,0,3:T(4,128)} %select_bitcast_fusion.6), channel_id=1, source_target_pairs={{0,1},{1,2},{2,3},{3,4},{4,5},{5,6},{6,7},{7,8},{8,9},{9,10},{10,1... | collective-permute-start | bytes 276488 | tf_op jit(solution)/shard_map/ppermute | solution.py:21
  304.9 2.5 copy-start.38
  307.4 5.8 %collective-permute-start.1 = (f32[10,72,4,8]{1,2,0,3:T(4,128)}, f32[10,72,4,8]{1,2,0,3:T(4,128)}, u32[]{:S(2)}, u32[]{:S(2)}) collective-permute-start(f32[10,72,4,8]{1,2,0,3:T(4,128)} %select_bitcast_fusion.5), channel_id=1, source_target_pairs={{0,31},{1,0},{2,1},{3,2},{4,3},{5,4},{6,5},{7,6},{8,7},{9,8},{10,9... | collective-permute-start | bytes 276488 | tf_op jit(solution)/shard_map/ppermute | solution.py:21
  316.0 1.9 copy-start.23
  320.6 2.4 copy-start.4
  334.2 2.3 copy-start.20
  340.6 9.3 %collective-permute-start.4 = (f32[10,72,4,8]{1,2,0,3:T(4,128)}, f32[10,72,4,8]{1,2,0,3:T(4,128)S(1)}, u32[]{:S(2)}, u32[]{:S(2)}) collective-permute-start(f32[10,72,4,8]{1,2,0,3:T(4,128)} %select_bitcast_fusion.4), channel_id=1, source_target_pairs={{0,1},{1,2},{2,3},{3,4},{4,5},{5,6},{6,7},{7,8},{8,9},{9,10},{10,1... | collective-permute-start | bytes 276488 | tf_op jit(solution)/shard_map/ppermute | solution.py:21
  357.8 5.5 %collective-permute-start.5 = (f32[10,72,4,8]{1,2,0,3:T(4,128)}, f32[10,72,4,8]{1,2,0,3:T(4,128)S(1)}, u32[]{:S(2)}, u32[]{:S(2)}) collective-permute-start(f32[10,72,4,8]{1,2,0,3:T(4,128)} %select_bitcast_fusion.3), channel_id=1, source_target_pairs={{0,31},{1,0},{2,1},{3,2},{4,3},{5,4},{6,5},{7,6},{8,7},{9,8},{10,9... | collective-permute-start | bytes 276488 | tf_op jit(solution)/shard_map/ppermute | solution.py:21
  365.1 1.9 copy-start.25
  369.5 2.4 copy-start.5
  390.6 8.6 %collective-permute-start.6 = (f32[10,72,4,8]{1,2,0,3:T(4,128)}, f32[10,72,4,8]{1,2,0,3:T(4,128)S(1)}, u32[]{:S(2)}, u32[]{:S(2)}) collective-permute-start(f32[10,72,4,8]{1,2,0,3:T(4,128)} %select_bitcast_fusion.2), channel_id=1, source_target_pairs={{0,1},{1,2},{2,3},{3,4},{4,5},{5,6},{6,7},{7,8},{8,9},{9,10},{10,1... | collective-permute-start | bytes 276488 | tf_op jit(solution)/shard_map/ppermute | solution.py:21
  407.0 5.5 %collective-permute-start.7 = (f32[10,72,4,8]{1,2,0,3:T(4,128)}, f32[10,72,4,8]{1,2,0,3:T(4,128)S(1)}, u32[]{:S(2)}, u32[]{:S(2)}) collective-permute-start(f32[10,72,4,8]{1,2,0,3:T(4,128)} %select_bitcast_fusion.1), channel_id=1, source_target_pairs={{0,31},{1,0},{2,1},{3,2},{4,3},{5,4},{6,5},{7,6},{8,7},{9,8},{10,9... | collective-permute-start | bytes 276488 | tf_op jit(solution)/shard_map/ppermute | solution.py:21
  (19 other events, 27.1 us)
where the time goes:
time: 429 us; the launch traced here: 421 us
  local copies, waits for them, and re-layouts  183 us (43%)
  other arithmetic  83.3 us (19%)
  matrix products  69.2 us (16%)
  waiting for transfers between devices  44.4 us (10%)
  starting transfers between devices  26.2 us (6%)
  loops' own time  12.6 us (3%)
    scatter x3, local copies, waits for them, and re-layouts, invert(): jnp.zeros((extent,), jnp.int32).at[permutation]  65.4 us
    ppermute x8, waiting for transfers between devices, from_behind(): lax.ppermute(array, axis, [(i, (i + by) % length) for i in range(length)])  44.3 us
    dot_general x20, matrix products, relax(): jnp.einsum('mx,xaq->maq', field_coupling_matrix, level_blended, precision...  27.4 us
    another operation x12, other arithmetic, combine(): jnp.stack([south_row + south_side, stepped[..., 1, :, :], stepped[..., 2,...  22.8 us
    dot_general x20, matrix products, relax(): jnp.einsum('flm,fmc->flc', level_mix, segment, precision=lax.Precision.HI...  15.9 us
    dot_general x3, matrix products, advect(): jnp.einsum('pq,...qe->...pe', upward, current, precision=lax.Precision.HI...  15.7 us
    another operation x1, loops' own time, advance_sorted(): return lax.fori_loop(0, 4 * SWEEPS, physics_pass, columns)  11.8 us
    dynamic_update_slice x20, other arithmetic, advance_block(): lax.dynamic_update_slice_in_dim(current, relax(segment, active, level_mix...  11.4 us
  transfers between devices with their start and end apart: 11, of which 7 were waited for; matrix products, arithmetic and copies ran while one was open for 31% of the time, Pallas kernels for 0%

commit v1 on v0

v1 whole, which is shorter than its diff:
```python
from functools import partial

import jax
import jax.numpy as jnp
import numpy as np
from jax import lax
from jax.experimental import pallas as pl
from jax.experimental.pallas import tpu as pltpu
from jax.sharding import PartitionSpec as P

ROWS_DEV = 4
SUBSTEPS = 3
SWEEPS = 4
CLASSES = 4
PHYSICS_RATE = 0.1
TIME_STEP = 0.02
AXES = ("elem", "face")
EXTRA = 8
F32, BF16 = jnp.float32, jnp.bfloat16
VMEM_LIMIT = 56 * 1024 * 1024

EAST_WEST, NORTH_SOUTH, SEND_UP, SEND_DOWN, FROM_NEXT, FROM_PREV, BY_CLASS, BY_SLOT, SLOT, COST = range(10)
TABLE_ROWS = 16


def derivative_matrix():
    nodes = np.array([-1.0, -1.0 / np.sqrt(5.0), 1.0 / np.sqrt(5.0), 1.0])
    derivative = np.zeros((4, 4))
    for i in range(4):
        for j in range(4):
            if i == j:
                derivative[i, j] = sum(1.0 / (nodes[j] - nodes[m]) for m in range(4) if m != j)
            else:
                top = np.prod([nodes[i] - nodes[m] for m in range(4) if m not in (i, j)])
                derivative[i, j] = top / np.prod([nodes[j] - nodes[m] for m in range(4) if m != j])
    return derivative


def derivative_operators(width):
    derivative = derivative_matrix()
    blocks = np.eye(width // 16)
    across = np.kron(blocks, np.kron(np.eye(4), derivative)).T
    upward = np.kron(blocks, np.kron(derivative, np.eye(4))).T
    both = np.concatenate([across, upward], axis=1).astype(np.float32)
    high = both.astype(jnp.bfloat16)
    low = (both - high.astype(np.float32)).astype(jnp.bfloat16)
    return high, low


def split(values):
    high = values.astype(BF16)
    return high, (values - high.astype(F32)).astype(BF16)


def nn(a, b):
    return jnp.dot(a, b, preferred_element_type=F32)


def nt(a, b):
    return lax.dot_general(a, b, (((1,), (1,)), ((), ())), preferred_element_type=F32)


def tn(a, b):
    return lax.dot_general(a, b, (((0,), (0,)), ((), ())), preferred_element_type=F32)


def onehot(row, count):
    picks = lax.broadcasted_iota(jnp.int32, (count, row.shape[1]), 0)
    return jnp.where(picks == row, 1.0, 0.0).astype(F32)


def physics_kernel(
    trips, table, state, mix, coupling, tendency, outgoing, gather_sum, send_rows, whi, wlo, wide, work
):
    rows, cols = state.shape
    levels = mix.shape[0]
    half = cols // 2

    def index(i):
        return table[i : i + 1, :]

    own = lax.broadcasted_iota(jnp.int32, (1, cols), 1)
    identity = onehot(own, cols)
    first = (identity + onehot(index(EAST_WEST), cols)).astype(BF16)
    second = (identity + onehot(index(NORTH_SOUTH), cols)).astype(BF16)
    gather_sum[...] = nn(first, second).astype(BF16)
    edge = send_rows.shape[0] // 2
    chosen = jnp.concatenate([onehot(index(SEND_UP), edge), onehot(index(SEND_DOWN), edge)], axis=0)
    send_rows[...] = nt(chosen.astype(BF16), first).astype(BF16)

    for g in range(rows // levels):
        wide[g * levels : (g + 1) * levels, :] = mix[...] * coupling[g : g + 1, :]
    high, low = split(wide[...])
    whi[...] = high
    wlo[...] = low

    order = onehot(index(BY_CLASS), cols).astype(BF16)
    xh, xl = split(state[...])
    begin = nt(xh, order) + nt(xl, order)
    tendency[...] = begin
    work[...] = begin
    bound = index(COST) * SWEEPS

    def step(width, k, carry):
        x = work[:, :width]
        high, low = split(x)
        y = nn(whi[...], high) + nn(whi[...], low) + nn(wlo[...], high)
        work[:, :width] = jnp.where(bound[:, :width] > k, x + PHYSICS_RATE * jnp.tanh(y), x)
        return carry

    lax.fori_loop(0, trips[0], partial(step, cols), 0)
    lax.fori_loop(trips[0], trips[1], partial(step, half), 0)

    high, low = split(work[...] - tendency[...])
    change = nn(high, order) + nn(low, order)
    tendency[...] = change
    slots = jnp.broadcast_to(index(SLOT).astype(F32), (EXTRA, cols))
    high, low = split(jnp.concatenate([state[...] + change, slots], axis=0))
    to_slot = onehot(index(BY_SLOT), cols).astype(BF16)
    outgoing[...] = nt(to_slot, high) + nt(to_slot, low)


def move(current, tendency, metric, dhi, dlo, gather_sum, send_rows, levels):
    rows, cols = current.shape
    width = dhi.shape[0]
    parts = []
    for start in range(0, cols, width):
        x = current[:, start : start + width]
        high, low = split(x)
        slopes = nn(high, dhi) + nn(low, dhi) + nn(high, dlo)
        u, v = x[:levels], x[levels : 2 * levels]
        fields = rows // levels
        u, v = jnp.concatenate([u] * fields, axis=0), jnp.concatenate([v] * fields, axis=0)
        parts.append(u * slopes[:, :width] + v * slopes[:, width:])
    rate = -jnp.concatenate(parts, axis=1)
    moved = current + TIME_STEP * rate + tendency / SUBSTEPS
    weighted = jnp.concatenate([metric * moved, jnp.broadcast_to(metric, (EXTRA, cols))], axis=0)
    high, low = split(weighted)
    return nn(high, gather_sum) + nn(low, gather_sum), nt(send_rows, high) + nt(send_rows, low)


def settle(local, from_next, from_prev, table, rows):
    edge = from_next.shape[0]
    place_next = onehot(table[FROM_NEXT : FROM_NEXT + 1, :], edge)
    place_prev = onehot(table[FROM_PREV : FROM_PREV + 1, :], edge)
    place = jnp.concatenate([place_next, place_prev], axis=0).astype(BF16)
    high, low = split(jnp.concatenate([from_next, from_prev], axis=0))
    total = local + tn(high, place) + tn(low, place)
    return total[:rows] / total[rows : rows + 1]


def first_kernel(levels, state, tendency, metric, dhi, dlo, gather_sum, send_rows, local, up, down):
    edge = up.shape[0]
    total, rows = move(
        state[...], tendency[...], metric[...], dhi[...], dlo[...], gather_sum[...], send_rows[...], levels
    )
    local[...] = total
    up[...] = rows[:edge]
    down[...] = rows[edge:]


def middle_kernel(
    levels, before, from_next, from_prev, table, tendency, metric, dhi, dlo, gather_sum, send_rows, local, up, down
):
    edge = up.shape[0]
    current = settle(before[...], from_next[...], from_prev[...], table[...], tendency.shape[0])
    total, rows = move(
        current, tendency[...], metric[...], dhi[...], dlo[...], gather_sum[...], send_rows[...], levels
    )
    local[...] = total
    up[...] = rows[:edge]
    down[...] = rows[edge:]


def last_kernel(before, from_next, from_prev, table, out):
    out[...] = settle(before[...], from_next[...], from_prev[...], table[...], out.shape[0])


def place_kernel(arrived, out):
    rows, cols = out.shape
    slot = arrived[:, rows : rows + 1]
    places = lax.broadcasted_iota(jnp.int32, (cols, cols), 1).astype(F32)
    put = jnp.where(places == slot, 1.0, 0.0).astype(BF16)
    high, low = split(arrived[:, :rows])
    out[...] = tn(high, put) + tn(low, put)


def shifted(array, by):
    length = lax.axis_size(AXES)
    return lax.ppermute(array, AXES, [(i, (i + by) % length) for i in range(length)])


def per_column(row, points):
    return jnp.broadcast_to(row[:, None], (row.shape[0], points)).reshape(-1)


def rank(keys, valid=None):
    smaller = keys[None, :] < keys[:, None]
    if valid is not None:
        smaller &= valid[None, :]
    return jnp.sum(smaller.astype(jnp.int32), axis=1)


def index_table(neighbours, classes, slots, points, myself):
    members = neighbours.shape[1]
    cols = members * points
    base = myself * members
    point = jnp.arange(cols, dtype=jnp.int32) % points
    ix, iy = point % 4, point // 4
    sequence = jnp.arange(members, dtype=jnp.int32)
    remote_up = neighbours[2] // members != myself
    remote_down = neighbours[3] // members != myself
    wide = partial(per_column, points=points)
    east, west, north, south = (wide(neighbours[i] - base) for i in range(4))
    up, down = wide(remote_up), wide(remote_down)
    top, bottom = iy == 3, iy == 0
    east_west = jnp.where(
        ix == 3, points * east + 4 * iy, jnp.where(ix == 0, points * west + 4 * iy + 3, -1)
    )
    north_south = jnp.where(
        top & ~up, points * north + ix, jnp.where(bottom & ~down, points * south + 12 + ix, -1)
    )
    send_up = jnp.where(top & up, 4 * wide(rank(sequence, remote_up)) + ix, -1)
    send_down = jnp.where(bottom & down, 4 * wide(rank(sequence, remote_down)) + ix, -1)
    from_next = jnp.where(top & up, 4 * wide(rank(neighbours[2], remote_up)) + ix, -1)
    from_prev = jnp.where(bottom & down, 4 * wide(rank(neighbours[3], remote_down)) + ix, -1)
    own = jnp.arange(cols, dtype=jnp.int32)
    by_class = rank(own - classes * cols)
    by_slot = rank(slots)
    counts = [jnp.sum((classes >= q).astype(jnp.int32)) for q in range(1, CLASSES + 1)]
    cost = sum((count > own).astype(jnp.int32) for count in counts)
    some = sum((count > cols // 2).astype(jnp.int32) for count in counts)
    most = sum((count > 0).astype(jnp.int32) for count in counts)
    trips = jnp.stack([some, most]) * SWEEPS
    rows = [east_west, north_south, send_up, send_down, from_next, from_prev, by_class, by_slot, slots % cols, cost]
    rows += [jnp.zeros_like(own)] * (TABLE_ROWS - len(rows))
    return jnp.stack(rows), trips


def call(kernel, out_shape, scratch=(), smem=0, inputs=1):
    vmem = pl.BlockSpec(memory_space=pltpu.VMEM)
    return pl.pallas_call(
        kernel,
        out_shape=out_shape,
        in_specs=[pl.BlockSpec(memory_space=pltpu.SMEM)] * smem + [vmem] * (inputs - smem),
        out_specs=jax.tree.map(lambda _: vmem, out_shape),
        scratch_shapes=list(scratch),
        compiler_params=pltpu.CompilerParams(vmem_limit_bytes=VMEM_LIMIT),
    )


def per_device(state, metric, neighbours, cost_class, batch_slot, level_mix, field_coupling_matrix):
    fields, levels, cols = state.shape
    points, members = metric.shape
    rows = fields * levels
    edge = 4 * (members // ROWS_DEV)
    myself = lax.axis_index(AXES)
    slots = lax.dynamic_slice_in_dim(batch_slot, myself * members, members, axis=1).T.reshape(cols)
    table, trips = index_table(neighbours, cost_class.T.reshape(cols), slots, points, myself)
    flat = state.reshape(rows, cols)
    weight = metric.T.reshape(1, cols)
    mix = jnp.transpose(level_mix, (1, 0, 2)).reshape(levels, rows)
    coupling = jnp.broadcast_to(field_coupling_matrix[:, :, None], (fields, fields, levels)).reshape(fields, rows)
    dhi, dlo = (jnp.asarray(m) for m in derivative_operators(min(cols, 256)))

    shape = jax.ShapeDtypeStruct
    tendency, outgoing, gather_sum, send_rows = call(
        physics_kernel,
        (
            shape((rows, cols), F32),
            shape((cols, rows + EXTRA), F32),
            shape((cols, cols), BF16),
            shape((2 * edge, cols), BF16),
        ),
        (
            pltpu.VMEM((rows, rows), BF16),
            pltpu.VMEM((rows, rows), BF16),
            pltpu.VMEM((rows, rows), F32),
            pltpu.VMEM((rows, cols), F32),
        ),
        smem=1,
        inputs=5,
    )(trips, table, flat, mix, coupling)
    arrived = lax.all_to_all(outgoing, AXES, split_axis=0, concat_axis=0, tiled=True)

    partly = (
        shape((rows + EXTRA, cols), F32),
        shape((edge, rows + EXTRA), F32),
        shape((edge, rows + EXTRA), F32),
    )
    fixed = (tendency, weight, dhi, dlo, gather_sum, send_rows)
    local, up, down = call(partial(first_kernel, levels), partly, inputs=7)(flat, *fixed)
    for _ in range(SUBSTEPS - 1):
        from_prev, from_next = shifted(up, 1), shifted(down, -1)
        local, up, down = call(partial(middle_kernel, levels), partly, inputs=10)(
            local, from_next, from_prev, table, *fixed
        )
    from_prev, from_next = shifted(up, 1), shifted(down, -1)
    out = call(last_kernel, shape((rows, cols), F32), inputs=4)(local, from_next, from_prev, table)
    physics = call(place_kernel, shape((rows, cols), F32), inputs=1)(arrived)
    return out.reshape(state.shape), physics.reshape(state.shape)


def solution(mesh):
    split_cols = P(None, AXES)
    return jax.shard_map(
        per_device,
        mesh=mesh,
        in_specs=(P(None, None, AXES), split_cols, split_cols, split_cols, P(), P(), P()),
        out_specs=(P(None, None, AXES), P(None, None, AXES)),
        check_vma=False,
    )
```

time: 429 us -> 141 us (0.33); the launches traced: 421 us -> 141 us
  local copies, waits for them, and re-layouts: 183 us -> 10.6 us
  other arithmetic: 83.3 us -> 8.62 us
  matrix products: 69.2 us -> 0 us
  Pallas kernels: 0 us -> 51.6 us
  loops' own time: 12.6 us -> 0 us
  waiting for transfers between devices: 44.4 us -> 37.4 us
    gather x47 -> x0, local copies, waits for them, and re-layouts: 73.9 us -> none  [the longest x5 9.88 us: cross_rows(): jnp.take(south_row, local_up, axis=-1)]
    dot_general x46 -> x0, matrix products: 69.2 us -> none  [the longest x20 27.4 us: relax(): jnp.einsum('mx,xaq->maq', field_coupling_matrix, level_blended, precision...]
    scatter x3 -> x0, local copies, waits for them, and re-layouts: 65.4 us -> none  [invert(): jnp.zeros((extent,), jnp.int32).at[permutation]]
    pallas_call x0 -> x6, Pallas kernels: none -> 51.6 us  [the longest x1 26.4 us: per_device(): call(physics_kernel, (shape((rows, cols), F32), shape((cols, rows + EXTRA...]
    another operation x17 -> x0, other arithmetic: 29.7 us -> none  [the longest x12 22.8 us: combine(): jnp.stack([south_row + south_side, stepped[..., 1, :, :], stepped[..., 2,...]
    another operation x17 -> x0, loops' own time: 12.6 us -> none  [the longest x1 11.8 us: advance_sorted(): return lax.fori_loop(0, 4 * SWEEPS, physics_pass, columns)]
    dynamic_update_slice x20 -> x0, other arithmetic: 11.4 us -> none  [advance_block(): lax.dynamic_update_slice_in_dim(current, relax(segment, active, level_mix...]
    sort x4 -> x0, other arithmetic: 10.8 us -> none  [the longest x1 3.77 us: per_device(): send_order = jnp.argsort(my_slots)]
  transfers between devices with their start and end apart: 11 -> 7, of which waited for: 7 -> 6; matrix products, arithmetic and copies ran while one was open for 31% -> 1% of each run, Pallas kernels for 0% -> 15%
where the time goes in v1:
time: 141 us
  Pallas kernels  51.6 us (37%)
  waiting for transfers between devices  37.4 us (27%)
  starting transfers between devices  26.8 us (19%)
  local copies, waits for them, and re-layouts  10.6 us (8%)
  other arithmetic  8.62 us (6%)
  between operations  5.89 us (4%)
    ppermute x6, waiting for transfers between devices, shifted(): lax.ppermute(array, AXES, [(i, (i + by) % length) for i in range(length)])  37.4 us
    pallas_call x1, Pallas kernels, per_device(): call(physics_kernel, (shape((rows, cols), F32), shape((cols, rows + EXTRA...  26.4 us
    ppermute x6, starting transfers between devices, shifted(): lax.ppermute(array, AXES, [(i, (i + by) % length) for i in range(length)])  13.9 us
    all_to_all x1, starting transfers between devices, per_device(): lax.all_to_all(outgoing, AXES, split_axis=0, concat_axis=0, tiled=True)  12.9 us
    pallas_call x2, Pallas kernels, per_device(): call(partial(middle_kernel, levels), partly, inputs=10)  12.5 us
    pallas_call x1, Pallas kernels, per_device(): call(partial(first_kernel, levels), partly, inputs=7)(flat, *fixed)  5.66 us
    pallas_call x1, Pallas kernels, per_device(): physics = call(place_kernel, shape((rows, cols), F32), inputs=1)(arrived)  3.55 us
    pallas_call x1, Pallas kernels, per_device(): call(last_kernel, shape((rows, cols), F32), inputs=4)  3.41 us
  transfers between devices with their start and end apart: 7, of which 6 were waited for; matrix products, arithmetic and copies ran while one was open for 1% of the time, Pallas kernels for 15%

profile of v1, /device:TPU:0, one launch (start us, length us, event | category | flops | bytes accessed | tf_op | source)
XLA Modules:
  0.0 140.8 jit_solution(7944383935916208909)
XLA Ops:
  0.7 0.8 fusion.6
  1.4 0.8 compare_bitcast_fusion
  2.2 0.8 subtract_multiply_fusion
  3.0 0.8 slice_bitcast_fusion
  4.1 1.5 %convert_reduce_fusion.6 = (s32[]{:T(128)}, s32[]{:T(128)}, s32[]{:T(128)}, s32[]{:T(128)}, s32[32,16]{0,1:T(8,128)S(1)}) fusion(s32[16,32]{1,0:T(8,128)} %param.12), kind=kLoop, calls=%fused_computation.13 | loop fusion | flops 6652 | bytes 4112 | tf_op jit(solution)/shard_map/reduce_sum | solution.py:230
  10.7 2.5 %fusion.4 = s32[1,512]{1,0:T(1,128)S(1)} fusion(s32[]{:T(128)} %get-tuple-element.28, s32[]{:T(128)} %get-tuple-element.29, s32[]{:T(128)} %get-tuple-element.30, s32[]{:T(128)} %get-tuple-element.31), kind=kLoop, calls=%fused_computation.36 | loop fusion | flops 5632 | bytes 2064 | tf_op jit(solution)/shard_map/add | solution.py:231
  15.8 0.8 broadcast_in_dim.39
  16.6 0.7 reshape.572.coupling
  17.3 1.1 copy.23
  18.4 0.8 copy.24.mix
  19.3 0.7 add_multiply_fusion.trips
  20.0 1.3 stack.39.table
  21.3 26.4 %shard_map.104 = (f32[720,512]{1,0:T(8,128)}, f32[512,728]{1,0:T(8,128)}, bf16[512,512]{1,0:T(8,128)(2,1)}, bf16[64,512]{1,0:T(8,128)(2,1)}) custom-call(s32[2]{0:T(128)} %add_multiply_fusion.trips, s32[16,512]{1,0:T(8,128)} %stack.39.table, f32[720,512]{1,0:T(8,128)} %bitcast.37, f32[72,720]{1,0:T(8,128)} %copy.24.mix, f32[10,720]{1,0:T(8,128)} %reshape.572.coupling), custom_call_target="tpu_custom_call" | custom-call | tf_op jit(solution)/shard_map/pallas_call | solution.py:267
  47.7 12.9 %all-to-all-start = ((f32[32,16,728]{2,1,0:T(8,128)}), f32[32,16,728]{2,1,0:T(8,128)S(1)}, u32[]{:S(2)}, u32[]{:S(2)}) async-start(f32[32,16,728]{2,1,0:T(8,128)} %bitcast.39), calls=%async_computation | async-start | bytes 3145728 | tf_op jit(solution)/shard_map/all_to_all | solution.py:284
  60.7 0.7 reshape.573.metric
  61.4 5.7 %shard_map.105 = (f32[728,512]{1,0:T(8,128)}, f32[32,728]{1,0:T(8,128)}, f32[32,728]{1,0:T(8,128)}) custom-call(f32[720,512]{1,0:T(8,128)} %bitcast.38, f32[720,512]{1,0:T(8,128)} %get-tuple-element.15.tendency, f32[1,512]{1,0:T(1,128)} %reshape.573.metric, bf16[256,512]{1,0:T(8,128)(2,1)} %constant.103.clone.dhi, bf16[256,512]{1,0:T(8,128)(2,1)} %constant.104.clone.dlo, ...), custom_call_target="tpu_custom_call" | custom-call | tf_op jit(solution)/shard_map/pallas_call | solution.py:292
  67.0 5.2 %collective-permute-start = (f32[32,728]{1,0:T(8,128)}, f32[32,728]{1,0:T(8,128)S(1)}, u32[]{:S(2)}, u32[]{:S(2)}) collective-permute-start(f32[32,728]{1,0:T(8,128)} %get-tuple-element.19), channel_id=1, source_target_pairs={{0,31},{1,0},{2,1},{3,2},{4,3},{5,4},{6,5},{7,6},{8,7},{9,8},{10,9... | collective-permute-start | bytes 279560 | tf_op jit(solution)/shard_map/ppermute | solution.py:190
  72.3 16.9 %collective-permute-done.from_next = f32[32,728]{1,0:T(8,128)S(1)} collective-permute-done((f32[32,728]{1,0:T(8,128)}, f32[32,728]{1,0:T(8,128)S(1)}, u32[]{:S(2)}, u32[]{:S(2)}) %collective-permute-start) | collective-permute-done | bytes 93216 | tf_op jit(solution)/shard_map/ppermute | solution.py:190
  89.2 7.1 %collective-permute-done.1.from_prev = f32[32,728]{1,0:T(8,128)S(1)} collective-permute-done((f32[32,728]{1,0:T(8,128)}, f32[32,728]{1,0:T(8,128)S(1)}, u32[]{:S(2)}, u32[]{:S(2)}) %collective-permute-start.1) | collective-permute-done | bytes 93216 | tf_op jit(solution)/shard_map/ppermute | solution.py:190
  96.3 0.6 copy-done.7
  96.9 6.2 %shard_map.106 = (f32[728,512]{1,0:T(8,128)}, f32[32,728]{1,0:T(8,128)}, f32[32,728]{1,0:T(8,128)}) custom-call(f32[728,512]{1,0:T(8,128)} %get-tuple-element.18.before, f32[32,728]{1,0:T(8,128)} %copy-done.6, f32[32,728]{1,0:T(8,128)} %copy-done.7, s32[16,512]{1,0:T(8,128)} %stack.39.table, f32[720,512]{1,0:T(8,128)} %get-tuple-element.15.tendency, ...), custom_call_target="tpu_custom_call" | custom-call | tf_op jit(solution)/shard_map/pallas_call | solution.py:295
  103.2 6.6 %collective-permute-start.3 = (f32[32,728]{1,0:T(8,128)}, f32[32,728]{1,0:T(8,128)S(1)}, u32[]{:S(2)}, u32[]{:S(2)}) collective-permute-start(f32[32,728]{1,0:T(8,128)} %get-tuple-element.23), channel_id=1, source_target_pairs={{0,1},{1,2},{2,3},{3,4},{4,5},{5,6},{6,7},{7,8},{8,9},{9,10},{10,1... | collective-permute-start | bytes 279560 | tf_op jit(solution)/shard_map/ppermute | solution.py:190
  109.8 2.8 %collective-permute-done.2.from_next = f32[32,728]{1,0:T(8,128)S(1)} collective-permute-done((f32[32,728]{1,0:T(8,128)}, f32[32,728]{1,0:T(8,128)S(1)}, u32[]{:S(2)}, u32[]{:S(2)}) %collective-permute-start.2) | collective-permute-done | bytes 93216 | tf_op jit(solution)/shard_map/ppermute | solution.py:190
  112.6 3.7 %collective-permute-done.3.from_prev = f32[32,728]{1,0:T(8,128)S(1)} collective-permute-done((f32[32,728]{1,0:T(8,128)}, f32[32,728]{1,0:T(8,128)S(1)}, u32[]{:S(2)}, u32[]{:S(2)}) %collective-permute-start.3) | collective-permute-done | bytes 93216 | tf_op jit(solution)/shard_map/ppermute | solution.py:190
  116.3 0.6 copy-done.5
  116.9 6.2 %shard_map.107 = (f32[728,512]{1,0:T(8,128)}, f32[32,728]{1,0:T(8,128)}, f32[32,728]{1,0:T(8,128)}) custom-call(f32[728,512]{1,0:T(8,128)} %get-tuple-element.21.before, f32[32,728]{1,0:T(8,128)} %copy-done.4, f32[32,728]{1,0:T(8,128)} %copy-done.5, s32[16,512]{1,0:T(8,128)} %stack.39.table, f32[720,512]{1,0:T(8,128)} %get-tuple-element.15.tendency, ...), custom_call_target="tpu_custom_call" | custom-call | tf_op jit(solution)/shard_map/pallas_call | solution.py:295
  123.2 2.0 %collective-permute-start.5 = (f32[32,728]{1,0:T(8,128)}, f32[32,728]{1,0:T(8,128)S(1)}, u32[]{:S(2)}, u32[]{:S(2)}) collective-permute-start(f32[32,728]{1,0:T(8,128)} %get-tuple-element.26), channel_id=1, source_target_pairs={{0,1},{1,2},{2,3},{3,4},{4,5},{5,6},{6,7},{7,8},{8,9},{9,10},{10,1... | collective-permute-start | bytes 279560 | tf_op jit(solution)/shard_map/ppermute | solution.py:190
  125.2 4.9 %collective-permute-done.4.from_next = f32[32,728]{1,0:T(8,128)S(1)} collective-permute-done((f32[32,728]{1,0:T(8,128)}, f32[32,728]{1,0:T(8,128)S(1)}, u32[]{:S(2)}, u32[]{:S(2)}) %collective-permute-start.4) | collective-permute-done | bytes 93216 | tf_op jit(solution)/shard_map/ppermute | solution.py:190
  130.1 2.0 %collective-permute-done.5.from_prev = f32[32,728]{1,0:T(8,128)S(1)} collective-permute-done((f32[32,728]{1,0:T(8,128)}, f32[32,728]{1,0:T(8,128)S(1)}, u32[]{:S(2)}, u32[]{:S(2)}) %collective-permute-start.5) | collective-permute-done | bytes 93216 | tf_op jit(solution)/shard_map/ppermute | solution.py:190
  132.7 3.4 %shard_map.108 = f32[720,512]{1,0:T(8,128)} custom-call(f32[728,512]{1,0:T(8,128)} %get-tuple-element.24.before, f32[32,728]{1,0:T(8,128)} %copy-done.2, f32[32,728]{1,0:T(8,128)} %copy-done.3, s32[16,512]{1,0:T(8,128)} %stack.39.table), custom_call_target="tpu_custom_call" | custom-call | tf_op jit(solution)/shard_map/pallas_call | solution.py:299
  136.1 1.2 copy-done.1
  137.3 3.5 %shard_map.109 = f32[720,512]{1,0:T(8,128)} custom-call(f32[512,728]{1,0:T(8,128)} %bitcast.36), custom_call_target="tpu_custom_call" | custom-call | tf_op jit(solution)/shard_map/pallas_call | solution.py:300
  (58 shorter events, 3.6 us)
Async XLA Ops:
  0.6 3.2 %copy-start = (s32[16,1024]{1,0:T(8,128)S(1)}, s32[16,1024]{1,0:T(8,128)}, u32[]{:S(2)}) copy-start(s32[16,1024]{1,0:T(8,128)} %param.13) | copy-start | bytes 196612
  47.7 12.9 %copy-start.8 = (f32[16,32]{1,0:T(8,128)S(1)}, f32[16,32]{1,0:T(8,128)}, u32[]{:S(2)}) copy-start(f32[16,32]{1,0:T(8,128)} %param.10) | copy-start | bytes 6148
  47.7 88.4 %all-to-all-start = ((f32[32,16,728]{2,1,0:T(8,128)}), f32[32,16,728]{2,1,0:T(8,128)S(1)}, u32[]{:S(2)}, u32[]{:S(2)}) async-start(f32[32,16,728]{2,1,0:T(8,128)} %bitcast.39), calls=%async_computation | async-start | bytes 3145728 | tf_op jit(solution)/shard_map/all_to_all | solution.py:284
  67.0 22.2 %collective-permute-start = (f32[32,728]{1,0:T(8,128)}, f32[32,728]{1,0:T(8,128)S(1)}, u32[]{:S(2)}, u32[]{:S(2)}) collective-permute-start(f32[32,728]{1,0:T(8,128)} %get-tuple-element.19), channel_id=1, source_target_pairs={{0,31},{1,0},{2,1},{3,2},{4,3},{5,4},{6,5},{7,6},{8,7},{9,8},{10,9... | collective-permute-start | bytes 279560 | tf_op jit(solution)/shard_map/ppermute | solution.py:190
  72.3 24.0 %collective-permute-start.1 = (f32[32,728]{1,0:T(8,128)}, f32[32,728]{1,0:T(8,128)S(1)}, u32[]{:S(2)}, u32[]{:S(2)}) collective-permute-start(f32[32,728]{1,0:T(8,128)} %get-tuple-element.20), channel_id=1, source_target_pairs={{0,1},{1,2},{2,3},{3,4},{4,5},{5,6},{6,7},{7,8},{8,9},{9,10},{10,1... | collective-permute-start | bytes 279560 | tf_op jit(solution)/shard_map/ppermute | solution.py:190
  89.2 7.1 %copy-start.6 = (f32[32,728]{1,0:T(8,128)}, f32[32,728]{1,0:T(8,128)S(1)}, u32[]{:S(2)}) copy-start(f32[32,728]{1,0:T(8,128)S(1)} %collective-permute-done.from_next) | copy-start | bytes 279556
  96.3 0.6 copy-start.7
  103.2 9.4 %collective-permute-start.2 = (f32[32,728]{1,0:T(8,128)}, f32[32,728]{1,0:T(8,128)S(1)}, u32[]{:S(2)}, u32[]{:S(2)}) collective-permute-start(f32[32,728]{1,0:T(8,128)} %get-tuple-element.22), channel_id=1, source_target_pairs={{0,31},{1,0},{2,1},{3,2},{4,3},{5,4},{6,5},{7,6},{8,7},{9,8},{10,9... | collective-permute-start | bytes 279560 | tf_op jit(solution)/shard_map/ppermute | solution.py:190
  103.2 13.1 %collective-permute-start.3 = (f32[32,728]{1,0:T(8,128)}, f32[32,728]{1,0:T(8,128)S(1)}, u32[]{:S(2)}, u32[]{:S(2)}) collective-permute-start(f32[32,728]{1,0:T(8,128)} %get-tuple-element.23), channel_id=1, source_target_pairs={{0,1},{1,2},{2,3},{3,4},{4,5},{5,6},{6,7},{7,8},{8,9},{9,10},{10,1... | collective-permute-start | bytes 279560 | tf_op jit(solution)/shard_map/ppermute | solution.py:190
  112.6 3.7 %copy-start.4 = (f32[32,728]{1,0:T(8,128)}, f32[32,728]{1,0:T(8,128)S(1)}, u32[]{:S(2)}) copy-start(f32[32,728]{1,0:T(8,128)S(1)} %collective-permute-done.2.from_next) | copy-start | bytes 279556
  116.3 0.6 copy-start.5
  123.2 6.9 %collective-permute-start.4 = (f32[32,728]{1,0:T(8,128)}, f32[32,728]{1,0:T(8,128)S(1)}, u32[]{:S(2)}, u32[]{:S(2)}) collective-permute-start(f32[32,728]{1,0:T(8,128)} %get-tuple-element.25), channel_id=1, source_target_pairs={{0,31},{1,0},{2,1},{3,2},{4,3},{5,4},{6,5},{7,6},{8,7},{9,8},{10,9... | collective-permute-start | bytes 279560 | tf_op jit(solution)/shard_map/ppermute | solution.py:190
  123.2 8.9 %collective-permute-start.5 = (f32[32,728]{1,0:T(8,128)}, f32[32,728]{1,0:T(8,128)S(1)}, u32[]{:S(2)}, u32[]{:S(2)}) collective-permute-start(f32[32,728]{1,0:T(8,128)} %get-tuple-element.26), channel_id=1, source_target_pairs={{0,1},{1,2},{2,3},{3,4},{4,5},{5,6},{6,7},{7,8},{8,9},{9,10},{10,1... | collective-permute-start | bytes 279560 | tf_op jit(solution)/shard_map/ppermute | solution.py:190
  130.1 2.0 %copy-start.2 = (f32[32,728]{1,0:T(8,128)}, f32[32,728]{1,0:T(8,128)S(1)}, u32[]{:S(2)}) copy-start(f32[32,728]{1,0:T(8,128)S(1)} %collective-permute-done.4.from_next) | copy-start | bytes 279556
  132.1 0.6 copy-start.3
  136.1 1.2 copy-start.1

commit v2 on v1

--- a/solution.py
+++ b/solution.py
@@ -116,7 +116,7 @@
     tendency[...] = change
     slots = jnp.broadcast_to(index(SLOT).astype(F32), (EXTRA, cols))
     high, low = split(jnp.concatenate([state[...] + change, slots], axis=0))
-    to_slot = onehot(index(BY_SLOT), cols).astype(BF16)
+    to_slot = onehot(index(BY_SLOT), outgoing.shape[0]).astype(BF16)
     outgoing[...] = nt(to_slot, high) + nt(to_slot, low)
 
 
@@ -149,45 +149,87 @@
     return total[:rows] / total[rows : rows + 1]
 
 
-def first_kernel(levels, state, tendency, metric, dhi, dlo, gather_sum, send_rows, local, up, down):
-    edge = up.shape[0]
-    total, rows = move(
-        state[...], tendency[...], metric[...], dhi[...], dlo[...], gather_sum[...], send_rows[...], levels
-    )
-    local[...] = total
-    up[...] = rows[:edge]
-    down[...] = rows[edge:]
-
-
-def middle_kernel(
-    levels, before, from_next, from_prev, table, tendency, metric, dhi, dlo, gather_sum, send_rows, local, up, down
+def exchange_kernel(
+    levels, per, state, tendency, metric, dhi, dlo, gather_sum, send_rows, table, outgoing, out, physics,
+    arrived, sent, received, near_send, near_recv, far_send, far_recv,
 ):
-    edge = up.shape[0]
-    current = settle(before[...], from_next[...], from_prev[...], table[...], tendency.shape[0])
-    total, rows = move(
-        current, tendency[...], metric[...], dhi[...], dlo[...], gather_sum[...], send_rows[...], levels
-    )
-    local[...] = total
-    up[...] = rows[:edge]
-    down[...] = rows[edge:]
-
-
-def last_kernel(before, from_next, from_prev, table, out):
-    out[...] = settle(before[...], from_next[...], from_prev[...], table[...], out.shape[0])
-
-
-def place_kernel(arrived, out):
     rows, cols = out.shape
+    edge = sent.shape[1] // 2
+    elems, faces = lax.axis_size("elem"), lax.axis_size("face")
+    devices = elems * faces
+    myself = lax.axis_index("elem") * faces + lax.axis_index("face")
+
+    def device(by):
+        other = lax.rem(myself + by, devices)
+        return other, (other // faces, lax.rem(other, faces))
+
+    barrier = pltpu.get_barrier_semaphore()
+
+    def greet(i, carry):
+        pl.semaphore_signal(barrier, inc=1, device_id=device(i)[1], device_id_type=pl.DeviceIdType.MESH)
+        return carry
+
+    lax.fori_loop(1, devices, greet, 0)
+
+    def near(step, way):
+        return pltpu.make_async_remote_copy(
+            src_ref=sent.at[step, pl.ds(way * edge, edge)],
+            dst_ref=received.at[step, pl.ds((1 - way) * edge, edge)],
+            send_sem=near_send.at[step, way],
+            recv_sem=near_recv.at[step, way],
+            device_id=device(1 if way == 0 else devices - 1)[1],
+            device_id_type=pl.DeviceIdType.MESH,
+        )
+
+    def far(i):
+        other, where = device(i)
+        return pltpu.make_async_remote_copy(
+            src_ref=outgoing.at[pl.ds(pl.multiple_of(other * per, 8), per)],
+            dst_ref=arrived.at[pl.ds(pl.multiple_of(myself * per, 8), per)],
+            send_sem=far_send.at[i],
+            recv_sem=far_recv.at[i],
+            device_id=where,
+            device_id_type=pl.DeviceIdType.MESH,
+        )
+
+    def start_far(i, carry):
+        far(i).start()
+        return carry
+
+    def wait_far(i, carry):
+        far(i).wait()
+        return carry
+
+    def advance(current):
+        return move(
+            current, tendency[...], metric[...], dhi[...], dlo[...], gather_sum[...], send_rows[...], levels
+        )
+
+    local, edges = advance(state[...])
+    sent[0] = edges
+    pl.semaphore_wait(barrier, devices - 1)
+    near(0, 0).start()
+    near(0, 1).start()
+    lax.fori_loop(1, devices, start_far, 0)
+    mine = pl.ds(pl.multiple_of(myself * per, 8), per)
+    arrived[mine, :] = outgoing[mine, :]
+    for step in range(SUBSTEPS):
+        near(step, 0).wait()
+        near(step, 1).wait()
+        current = settle(local, received[step, :edge], received[step, edge:], table[...], rows)
+        if step < SUBSTEPS - 1:
+            local, edges = advance(current)
+            sent[step + 1] = edges
+            near(step + 1, 0).start()
+            near(step + 1, 1).start()
+        else:
+            out[...] = current
+    lax.fori_loop(1, devices, wait_far, 0)
     slot = arrived[:, rows : rows + 1]
-    places = lax.broadcasted_iota(jnp.int32, (cols, cols), 1).astype(F32)
+    places = lax.broadcasted_iota(jnp.int32, (arrived.shape[0], cols), 1).astype(F32)
     put = jnp.where(places == slot, 1.0, 0.0).astype(BF16)
     high, low = split(arrived[:, :rows])
-    out[...] = tn(high, put) + tn(low, put)
-
-
-def shifted(array, by):
-    length = lax.axis_size(AXES)
-    return lax.ppermute(array, AXES, [(i, (i + by) % length) for i in range(length)])
+    physics[...] = tn(high, put) + tn(low, put)
 
 
 def per_column(row, points):
@@ -201,7 +243,7 @@
     return jnp.sum(smaller.astype(jnp.int32), axis=1)
 
 
-def index_table(neighbours, classes, slots, points, myself):
+def index_table(neighbours, classes, slots, points, myself, per):
     members = neighbours.shape[1]
     cols = members * points
     base = myself * members
@@ -227,6 +269,8 @@
     own = jnp.arange(cols, dtype=jnp.int32)
     by_class = rank(own - classes * cols)
     by_slot = rank(slots)
+    pair = cols // lax.axis_size(AXES)
+    by_slot = by_slot // pair * per + by_slot % pair
     counts = [jnp.sum((classes >= q).astype(jnp.int32)) for q in range(1, CLASSES + 1)]
     cost = sum((count > own).astype(jnp.int32) for count in counts)
     some = sum((count > cols // 2).astype(jnp.int32) for count in counts)
@@ -237,7 +281,7 @@
     return jnp.stack(rows), trips
 
 
-def call(kernel, out_shape, scratch=(), smem=0, inputs=1):
+def call(kernel, out_shape, scratch=(), smem=0, inputs=1, **params):
     vmem = pl.BlockSpec(memory_space=pltpu.VMEM)
     return pl.pallas_call(
         kernel,
@@ -245,7 +289,7 @@
         in_specs=[pl.BlockSpec(memory_space=pltpu.SMEM)] * smem + [vmem] * (inputs - smem),
         out_specs=jax.tree.map(lambda _: vmem, out_shape),
         scratch_shapes=list(scratch),
-        compiler_params=pltpu.CompilerParams(vmem_limit_bytes=VMEM_LIMIT),
+        compiler_params=pltpu.CompilerParams(vmem_limit_bytes=VMEM_LIMIT, **params),
     )
 
 
@@ -255,8 +299,10 @@
     rows = fields * levels
     edge = 4 * (members // ROWS_DEV)
     myself = lax.axis_index(AXES)
+    devices = lax.axis_size(AXES)
+    per = -(-(cols // devices) // 8) * 8
     slots = lax.dynamic_slice_in_dim(batch_slot, myself * members, members, axis=1).T.reshape(cols)
-    table, trips = index_table(neighbours, cost_class.T.reshape(cols), slots, points, myself)
+    table, trips = index_table(neighbours, cost_class.T.reshape(cols), slots, points, myself, per)
     flat = state.reshape(rows, cols)
     weight = metric.T.reshape(1, cols)
     mix = jnp.transpose(level_mix, (1, 0, 2)).reshape(levels, rows)
@@ -268,7 +314,7 @@
         physics_kernel,
         (
             shape((rows, cols), F32),
-            shape((cols, rows + EXTRA), F32),
+            shape((devices * per, rows + EXTRA), F32),
             shape((cols, cols), BF16),
             shape((2 * edge, cols), BF16),
         ),
@@ -281,23 +327,22 @@
         smem=1,
         inputs=5,
     )(trips, table, flat, mix, coupling)
-    arrived = lax.all_to_all(outgoing, AXES, split_axis=0, concat_axis=0, tiled=True)
-
-    partly = (
-        shape((rows + EXTRA, cols), F32),
-        shape((edge, rows + EXTRA), F32),
-        shape((edge, rows + EXTRA), F32),
-    )
-    fixed = (tendency, weight, dhi, dlo, gather_sum, send_rows)
-    local, up, down = call(partial(first_kernel, levels), partly, inputs=7)(flat, *fixed)
-    for _ in range(SUBSTEPS - 1):
-        from_prev, from_next = shifted(up, 1), shifted(down, -1)
-        local, up, down = call(partial(middle_kernel, levels), partly, inputs=10)(
-            local, from_next, from_prev, table, *fixed
-        )
-    from_prev, from_next = shifted(up, 1), shifted(down, -1)
-    out = call(last_kernel, shape((rows, cols), F32), inputs=4)(local, from_next, from_prev, table)
-    physics = call(place_kernel, shape((rows, cols), F32), inputs=1)(arrived)
+    out, physics = call(
+        partial(exchange_kernel, levels, per),
+        (shape((rows, cols), F32), shape((rows, cols), F32)),
+        (
+            pltpu.VMEM((devices * per, rows + EXTRA), F32),
+            pltpu.VMEM((SUBSTEPS, 2 * edge, rows + EXTRA), F32),
+            pltpu.VMEM((SUBSTEPS, 2 * edge, rows + EXTRA), F32),
+            pltpu.SemaphoreType.DMA((SUBSTEPS, 2)),
+            pltpu.SemaphoreType.DMA((SUBSTEPS, 2)),
+            pltpu.SemaphoreType.DMA((devices,)),
+            pltpu.SemaphoreType.DMA((devices,)),
+        ),
+        inputs=9,
+        collective_id=0,
+        has_side_effects=True,
+    )(flat, tendency, weight, dhi, dlo, gather_sum, send_rows, table, outgoing)
     return out.reshape(state.shape), physics.reshape(state.shape)
 
 

time: 141 us -> 122 us (0.87)
  Pallas kernels: 51.6 us -> 94.5 us
  waiting for transfers between devices: 37.4 us -> 0 us
  starting transfers between devices: 26.8 us -> 0 us
    pallas_call x6 -> x2, Pallas kernels: 51.6 us -> 94.5 us  [the longest x1 79.8 us: per_device(): call(partial(exchange_kernel, levels, per), (shape((rows, cols), F32), sh...]
    ppermute x6 -> x0, waiting for transfers between devices: 37.4 us -> none  [shifted(): lax.ppermute(array, AXES, [(i, (i + by) % length) for i in range(length)])]
    ppermute x6 -> x0, starting transfers between devices: 13.9 us -> none  [shifted(): lax.ppermute(array, AXES, [(i, (i + by) % length) for i in range(length)])]
    all_to_all x1 -> x0, starting transfers between devices: 12.9 us -> none  [per_device(): lax.all_to_all(outgoing, AXES, split_axis=0, concat_axis=0, tiled=True)]
    unnamed x18 -> x6, local copies, waits for them, and re-layouts: 3.07 us -> 3.83 us
  transfers between devices with their start and end apart: 7 -> 0, of which waited for: 6 -> 0; matrix products, arithmetic and copies ran while one was open for 1% -> 0% of each run, Pallas kernels for 15% -> 0%
where the time goes in v2:
time: 122 us; the launch traced here: 121 us
  Pallas kernels  94.5 us (77%)
  local copies, waits for them, and re-layouts  12 us (10%)
  other arithmetic  8.64 us (7%)
  between operations  5.88 us (5%)
    pallas_call x1, Pallas kernels, per_device(): call(partial(exchange_kernel, levels, per), (shape((rows, cols), F32), sh...  79.8 us
    pallas_call x1, Pallas kernels, per_device(): call(physics_kernel, (shape((rows, cols), F32), shape((devices * per, row...  14.8 us
    unnamed x6, local copies, waits for them, and re-layouts  3.83 us
    add x1, other arithmetic, index_table(): by_slot = by_slot // pair * per + by_slot % pair  2.56 us

profile of v2, /device:TPU:0, one launch (start us, length us, event | category | flops | bytes accessed | tf_op | source)
XLA Modules:
  0.0 121.1 jit_solution(1112576091346878167)
XLA Ops:
  0.7 0.8 fusion.7
  1.4 0.8 compare_bitcast_fusion
  2.2 0.8 subtract_multiply_fusion
  3.0 0.8 slice_bitcast_fusion
  3.8 0.2 convert_reduce_fusion.2
  4.1 0.1 reshape.641
  4.3 0.1 reshape.640
  4.6 0.1 reshape.642
  4.7 0.3 convert_reduce_fusion
  5.0 1.5 %convert_reduce_fusion.6 = (s32[]{:T(128)}, s32[]{:T(128)}, s32[]{:T(128)}, s32[]{:T(128)}, s32[32,16]{0,1:T(8,128)S(1)}) fusion(s32[16,32]{1,0:T(8,128)} %param.12), kind=kLoop, calls=%fused_computation.13 | loop fusion | flops 6652 | bytes 4112 | tf_op jit(solution)/shard_map/reduce_sum | solution.py:274
  11.5 0.7 add_multiply_fusion.trips
  12.2 2.6 %fusion.2 = (s32[1,512]{1,0:T(1,128)S(1)}, s32[1,512]{1,0:T(1,128)S(1)}) fusion(s32[1,512]{1,0:T(1,128)S(1)} %bitcast.42, s32[]{:T(128)} %get-tuple-element.14, s32[]{:T(128)} %get-tuple-element.15, s32[]{:T(128)} %get-tuple-element.16, s32[]{:T(128)} %get-tuple-element.17), kind=kLoop, calls=%fused_computation.39 | loop fusion | flops 16384 | bytes 6160 | tf_op jit(solution)/shard_map/add | solution.py:273
  14.9 0.3 convert_reduce_fusion.1
  15.3 0.1 mul.189
  15.4 0.1 mul.185
  15.6 0.1 mul.187
  15.7 0.1 mul.191
  15.9 0.1 mul.182
  16.0 0.1 mul.180
  16.2 0.1 mul.176
  16.4 0.1 add.360
  16.5 1.2 %stack.36.table = s32[16,512]{1,0:T(8,128)} concatenate(s32[1,512]{1,0:T(1,128)S(1)} %get-tuple-element.41, s32[1,512]{1,0:T(1,128)S(1)} %get-tuple-element.25, s32[1,512]{1,0:T(1,128)S(1)} %get-tuple-element.27, s32[1,512]{1,0:T(1,128)S(1)} %get-tuple-element.24, s32[1,512]{1,0:T(1,128)S(1)} %get-tuple-element.26, s32[1,512]{1,0:T(1,128)S(1)} %get-tuple-element.23, ...), dimensions={0} | concatenate | bytes 65536 | tf_op jit(solution)/shard_map/stack | solution.py:281
  17.8 0.8 copy.25
  18.6 0.7 reshape.645.metric
  19.2 0.8 broadcast_in_dim.39
  20.0 0.7 reshape.644.coupling
  20.7 1.1 copy.23
  21.9 0.8 copy.24.mix
  22.7 14.8 %shard_map.104 = (f32[720,512]{1,0:T(8,128)}, f32[512,728]{1,0:T(8,128)}, bf16[512,512]{1,0:T(8,128)(2,1)}, bf16[64,512]{1,0:T(8,128)(2,1)}) custom-call(s32[2]{0:T(128)} %add_multiply_fusion.trips, s32[16,512]{1,0:T(8,128)} %stack.36.table, f32[720,512]{1,0:T(8,128)} %bitcast.34, f32[72,720]{1,0:T(8,128)} %copy.24.mix, f32[10,720]{1,0:T(8,128)} %reshape.644.coupling), custom_call_target="tpu_custom_call" | custom-call | tf_op jit(solution)/shard_map/pallas_call | solution.py:313
  37.5 79.8 %shard_map.105 = (f32[720,512]{1,0:T(8,128)}, f32[720,512]{1,0:T(8,128)}) custom-call(f32[720,512]{1,0:T(8,128)} %bitcast.35, f32[720,512]{1,0:T(8,128)} %get-tuple-element.8.tendency, f32[1,512]{1,0:T(1,128)} %reshape.645.metric, bf16[256,512]{1,0:T(8,128)(2,1)} %constant.116.clone.dhi, bf16[256,512]{1,0:T(8,128)(2,1)} %constant.117.clone.dlo, ...), custom_call_target="tpu_custom_call" | custom-call | tf_op jit(solution)/shard_map/pallas_call | solution.py:330
  117.3 2.7 %copy.28 = f32[10,72,512]{2,1,0:T(8,128)} copy(f32[10,72,512]{2,1,0:T(8,128)} %bitcast.37) | data formatting | bytes 2949120
  120.0 1.1 copy.29
  (28 shorter events, 1.2 us)
Async XLA Ops:
  0.6 3.8 %copy-start = (s32[16,1024]{1,0:T(8,128)S(1)}, s32[16,1024]{1,0:T(8,128)}, u32[]{:S(2)}) copy-start(s32[16,1024]{1,0:T(8,128)} %param.13) | copy-start | bytes 196612
  117.2 2.7 %copy-start.1 = (f32[720,512]{1,0:T(8,128)S(1)}, f32[720,512]{1,0:T(8,128)}, u32[]{:S(2)}) copy-start(f32[720,512]{1,0:T(8,128)} %get-tuple-element.13) | copy-start | bytes 4423684

commit v3 on v2

--- a/solution.py
+++ b/solution.py
@@ -19,8 +19,9 @@
 F32, BF16 = jnp.float32, jnp.bfloat16
 VMEM_LIMIT = 56 * 1024 * 1024
 
-EAST_WEST, NORTH_SOUTH, SEND_UP, SEND_DOWN, FROM_NEXT, FROM_PREV, BY_CLASS, BY_SLOT, SLOT, COST = range(10)
-TABLE_ROWS = 16
+FROM_NEXT, FROM_PREV, WEIGHT = range(3)
+TABLE_ROWS = 8
+FAR_AWAY = float(2**24)
 
 
 def derivative_matrix():
@@ -65,58 +66,146 @@
 
 
 def onehot(row, count):
-    picks = lax.broadcasted_iota(jnp.int32, (count, row.shape[1]), 0)
+    picks = lax.broadcasted_iota(jnp.int32, (count, row.shape[1]), 0).astype(F32)
     return jnp.where(picks == row, 1.0, 0.0).astype(F32)
 
 
+def exact(a, b):
+    return jnp.dot(a, b, precision=lax.Precision.HIGHEST, preferred_element_type=F32)
+
+
+def index_rows(metric, neighbours, classes, slots):
+    points, members = metric.shape
+    cols = points * members
+    base = ((lax.axis_index("elem") * lax.axis_size("face") + lax.axis_index("face")) * members).astype(F32)
+    shift = points.bit_length() - 1
+    own = lax.broadcasted_iota(jnp.int32, (1, cols), 1)
+    element, point = (own >> shift).astype(F32), own & (points - 1)
+    ix, iy = (point & 3).astype(F32), (point >> 2).astype(F32)
+    leading = point == 0
+    sequence = own.astype(F32)
+    stacked = jnp.concatenate([metric, classes.astype(F32), slots.astype(F32)], axis=0)
+    spread = onehot(element, members)
+    rows = exact(stacked, spread)
+    mine = lax.broadcasted_iota(jnp.int32, (points, cols), 0) == point
+    weight, cost, slot = (
+        jnp.sum(jnp.where(mine, rows[i * points : (i + 1) * points], 0.0), axis=0, keepdims=True) for i in range(3)
+    )
+    near = exact(neighbours.astype(F32), spread) - base
+    east, west, north, south = (near[i : i + 1] for i in range(4))
+    up = (north < 0.0) | (north >= members)
+    down = (south < 0.0) | (south >= members)
+    top, bottom = iy == 3.0, iy == 0.0
+
+    keys = jnp.concatenate(
+        [
+            sequence - cost * cols,
+            slot,
+            jnp.where(up & leading, element, FAR_AWAY),
+            jnp.where(down & leading, element, FAR_AWAY),
+            jnp.where(up & leading, north, FAR_AWAY),
+            jnp.where(down & leading, south, FAR_AWAY),
+            sequence,
+            sequence,
+        ],
+        axis=0,
+    )
+    turned = jnp.transpose(keys)
+
+    def rank(i, values):
+        return jnp.sum(jnp.where(turned[:, i : i + 1] < values, 1.0, 0.0), axis=0, keepdims=True)
+
+    east_west = jnp.where(
+        ix == 3.0, points * east + 4.0 * iy, jnp.where(ix == 0.0, points * west + 4.0 * iy + 3.0, -1.0)
+    )
+    north_south = jnp.where(
+        top & ~up, points * north + ix, jnp.where(bottom & ~down, points * south + 12.0 + ix, -1.0)
+    )
+    send_up = jnp.where(top & up, 4.0 * rank(2, element) + ix, -1.0)
+    send_down = jnp.where(bottom & down, 4.0 * rank(3, element) + ix, -1.0)
+    from_next = jnp.where(top & up, 4.0 * rank(4, north) + ix, -1.0)
+    from_prev = jnp.where(bottom & down, 4.0 * rank(5, south) + ix, -1.0)
+    ordered = jnp.zeros((1, cols), F32)
+    for q in range(1, CLASSES + 1):
+        count = jnp.sum(jnp.where(cost >= q, 1.0, 0.0), axis=1, keepdims=True)
+        ordered += jnp.where(sequence < count, 1.0, 0.0)
+    return {
+        "east_west": east_west,
+        "north_south": north_south,
+        "send_up": send_up,
+        "send_down": send_down,
+        "from_next": from_next,
+        "from_prev": from_prev,
+        "by_class": rank(0, keys[0:1]),
+        "by_slot": rank(1, slot),
+        "slot": slot,
+        "weight": weight,
+        "bound": ordered * SWEEPS,
+    }
+
+
 def physics_kernel(
-    trips, table, state, mix, coupling, tendency, outgoing, gather_sum, send_rows, whi, wlo, wide, work
+    per, state, metric, neighbours, classes, slots, mix, coupling,
+    tendency, outgoing, gather_sum, send_rows, table, whi, wlo, wide, work, spreadmix,
 ):
     rows, cols = state.shape
-    levels = mix.shape[0]
+    fields, levels, _ = mix.shape
     half = cols // 2
-
-    def index(i):
-        return table[i : i + 1, :]
-
-    own = lax.broadcasted_iota(jnp.int32, (1, cols), 1)
+    index = index_rows(metric[...], neighbours[...], classes[...], slots[...])
+    blank = jnp.zeros((TABLE_ROWS - 3, cols), F32)
+    table[...] = jnp.concatenate([index["from_next"], index["from_prev"], index["weight"], blank], axis=0)
+
+    own = lax.broadcasted_iota(jnp.int32, (1, cols), 1).astype(F32)
     identity = onehot(own, cols)
-    first = (identity + onehot(index(EAST_WEST), cols)).astype(BF16)
-    second = (identity + onehot(index(NORTH_SOUTH), cols)).astype(BF16)
+    first = (identity + onehot(index["east_west"], cols)).astype(BF16)
+    second = (identity + onehot(index["north_south"], cols)).astype(BF16)
     gather_sum[...] = nn(first, second).astype(BF16)
     edge = send_rows.shape[0] // 2
-    chosen = jnp.concatenate([onehot(index(SEND_UP), edge), onehot(index(SEND_DOWN), edge)], axis=0)
+    chosen = jnp.concatenate([onehot(index["send_up"], edge), onehot(index["send_down"], edge)], axis=0)
     send_rows[...] = nt(chosen.astype(BF16), first).astype(BF16)
 
-    for g in range(rows // levels):
-        wide[g * levels : (g + 1) * levels, :] = mix[...] * coupling[g : g + 1, :]
+    place = lax.broadcasted_iota(jnp.int32, (fields, rows), 1)
+    field = lax.broadcasted_iota(jnp.int32, (fields, rows), 0)
+    inside = (place >= field * levels) & (place < (field + 1) * levels)
+    gains = exact(coupling[...], jnp.where(inside, 1.0, 0.0))
+    for f in range(fields):
+        spreadmix[:, f * levels : (f + 1) * levels] = mix[f]
+    for g in range(fields):
+        wide[g * levels : (g + 1) * levels, :] = spreadmix[...] * gains[g : g + 1, :]
     high, low = split(wide[...])
     whi[...] = high
     wlo[...] = low
 
-    order = onehot(index(BY_CLASS), cols).astype(BF16)
+    order = onehot(index["by_class"], cols).astype(BF16)
     xh, xl = split(state[...])
     begin = nt(xh, order) + nt(xl, order)
     tendency[...] = begin
     work[...] = begin
-    bound = index(COST) * SWEEPS
+    bound = index["bound"]
+    later = jnp.where(own >= half, bound, 0.0)
+    most, some = jnp.max(bound).astype(jnp.int32), jnp.max(later).astype(jnp.int32)
 
     def step(width, k, carry):
         x = work[:, :width]
         high, low = split(x)
         y = nn(whi[...], high) + nn(whi[...], low) + nn(wlo[...], high)
-        work[:, :width] = jnp.where(bound[:, :width] > k, x + PHYSICS_RATE * jnp.tanh(y), x)
+        work[:, :width] = jnp.where(bound[:, :width] > k.astype(F32), x + PHYSICS_RATE * jnp.tanh(y), x)
         return carry
 
-    lax.fori_loop(0, trips[0], partial(step, cols), 0)
-    lax.fori_loop(trips[0], trips[1], partial(step, half), 0)
+    lax.fori_loop(0, some, partial(step, cols), 0)
+    lax.fori_loop(some, most, partial(step, half), 0)
 
     high, low = split(work[...] - tendency[...])
     change = nn(high, order) + nn(low, order)
     tendency[...] = change
-    slots = jnp.broadcast_to(index(SLOT).astype(F32), (EXTRA, cols))
+    slots = jnp.broadcast_to(index["slot"], (EXTRA, cols))
     high, low = split(jnp.concatenate([state[...] + change, slots], axis=0))
-    to_slot = onehot(index(BY_SLOT), outgoing.shape[0]).astype(BF16)
+    spot = index["by_slot"]
+    pair = cols // (outgoing.shape[0] // per)
+    if pair != per:
+        whole = spot.astype(jnp.int32)
+        spot = (lax.div(whole, pair) * per + lax.rem(whole, pair)).astype(F32)
+    to_slot = onehot(spot, outgoing.shape[0]).astype(BF16)
     outgoing[...] = nt(to_slot, high) + nt(to_slot, low)
 
 
@@ -150,7 +239,7 @@
 
 
 def exchange_kernel(
-    levels, per, state, tendency, metric, dhi, dlo, gather_sum, send_rows, table, outgoing, out, physics,
+    levels, per, state, tendency, dhi, dlo, gather_sum, send_rows, table, outgoing, out, physics,
     arrived, sent, received, near_send, near_recv, far_send, far_recv,
 ):
     rows, cols = out.shape
@@ -202,7 +291,7 @@
 
     def advance(current):
         return move(
-            current, tendency[...], metric[...], dhi[...], dlo[...], gather_sum[...], send_rows[...], levels
+            current, tendency[...], table[WEIGHT : WEIGHT + 1, :], dhi[...], dlo[...], gather_sum[...], send_rows[...], levels
         )
 
     local, edges = advance(state[...])
@@ -210,7 +299,8 @@
     pl.semaphore_wait(barrier, devices - 1)
     near(0, 0).start()
     near(0, 1).start()
-    lax.fori_loop(1, devices, start_far, 0)
+    cuts = [1, 1 + (devices - 1) // 4, 1 + (devices - 1) // 2, devices]
+    lax.fori_loop(cuts[0], cuts[1], start_far, 0)
     mine = pl.ds(pl.multiple_of(myself * per, 8), per)
     arrived[mine, :] = outgoing[mine, :]
     for step in range(SUBSTEPS):
@@ -222,71 +312,23 @@
             sent[step + 1] = edges
             near(step + 1, 0).start()
             near(step + 1, 1).start()
+            lax.fori_loop(cuts[step + 1], cuts[step + 2], start_far, 0)
         else:
             out[...] = current
     lax.fori_loop(1, devices, wait_far, 0)
     slot = arrived[:, rows : rows + 1]
     places = lax.broadcasted_iota(jnp.int32, (arrived.shape[0], cols), 1).astype(F32)
-    put = jnp.where(places == slot, 1.0, 0.0).astype(BF16)
+    put = jnp.where(places == slot - (myself * cols).astype(F32), 1.0, 0.0).astype(BF16)
     high, low = split(arrived[:, :rows])
     physics[...] = tn(high, put) + tn(low, put)
 
 
-def per_column(row, points):
-    return jnp.broadcast_to(row[:, None], (row.shape[0], points)).reshape(-1)
-
-
-def rank(keys, valid=None):
-    smaller = keys[None, :] < keys[:, None]
-    if valid is not None:
-        smaller &= valid[None, :]
-    return jnp.sum(smaller.astype(jnp.int32), axis=1)
-
-
-def index_table(neighbours, classes, slots, points, myself, per):
-    members = neighbours.shape[1]
-    cols = members * points
-    base = myself * members
-    point = jnp.arange(cols, dtype=jnp.int32) % points
-    ix, iy = point % 4, point // 4
-    sequence = jnp.arange(members, dtype=jnp.int32)
-    remote_up = neighbours[2] // members != myself
-    remote_down = neighbours[3] // members != myself
-    wide = partial(per_column, points=points)
-    east, west, north, south = (wide(neighbours[i] - base) for i in range(4))
-    up, down = wide(remote_up), wide(remote_down)
-    top, bottom = iy == 3, iy == 0
-    east_west = jnp.where(
-        ix == 3, points * east + 4 * iy, jnp.where(ix == 0, points * west + 4 * iy + 3, -1)
-    )
-    north_south = jnp.where(
-        top & ~up, points * north + ix, jnp.where(bottom & ~down, points * south + 12 + ix, -1)
-    )
-    send_up = jnp.where(top & up, 4 * wide(rank(sequence, remote_up)) + ix, -1)
-    send_down = jnp.where(bottom & down, 4 * wide(rank(sequence, remote_down)) + ix, -1)
-    from_next = jnp.where(top & up, 4 * wide(rank(neighbours[2], remote_up)) + ix, -1)
-    from_prev = jnp.where(bottom & down, 4 * wide(rank(neighbours[3], remote_down)) + ix, -1)
-    own = jnp.arange(cols, dtype=jnp.int32)
-    by_class = rank(own - classes * cols)
-    by_slot = rank(slots)
-    pair = cols // lax.axis_size(AXES)
-    by_slot = by_slot // pair * per + by_slot % pair
-    counts = [jnp.sum((classes >= q).astype(jnp.int32)) for q in range(1, CLASSES + 1)]
-    cost = sum((count > own).astype(jnp.int32) for count in counts)
-    some = sum((count > cols // 2).astype(jnp.int32) for count in counts)
-    most = sum((count > 0).astype(jnp.int32) for count in counts)
-    trips = jnp.stack([some, most]) * SWEEPS
-    rows = [east_west, north_south, send_up, send_down, from_next, from_prev, by_class, by_slot, slots % cols, cost]
-    rows += [jnp.zeros_like(own)] * (TABLE_ROWS - len(rows))
-    return jnp.stack(rows), trips
-
-
-def call(kernel, out_shape, scratch=(), smem=0, inputs=1, **params):
+def call(kernel, out_shape, scratch=(), inputs=1, **params):
     vmem = pl.BlockSpec(memory_space=pltpu.VMEM)
     return pl.pallas_call(
         kernel,
         out_shape=out_shape,
-        in_specs=[pl.BlockSpec(memory_space=pltpu.SMEM)] * smem + [vmem] * (inputs - smem),
+        in_specs=[vmem] * inputs,
         out_specs=jax.tree.map(lambda _: vmem, out_shape),
         scratch_shapes=list(scratch),
         compiler_params=pltpu.CompilerParams(vmem_limit_bytes=VMEM_LIMIT, **params),
@@ -301,32 +343,29 @@
     myself = lax.axis_index(AXES)
     devices = lax.axis_size(AXES)
     per = -(-(cols // devices) // 8) * 8
-    slots = lax.dynamic_slice_in_dim(batch_slot, myself * members, members, axis=1).T.reshape(cols)
-    table, trips = index_table(neighbours, cost_class.T.reshape(cols), slots, points, myself, per)
+    slots = lax.dynamic_slice_in_dim(batch_slot, myself * members, members, axis=1)
     flat = state.reshape(rows, cols)
-    weight = metric.T.reshape(1, cols)
-    mix = jnp.transpose(level_mix, (1, 0, 2)).reshape(levels, rows)
-    coupling = jnp.broadcast_to(field_coupling_matrix[:, :, None], (fields, fields, levels)).reshape(fields, rows)
     dhi, dlo = (jnp.asarray(m) for m in derivative_operators(min(cols, 256)))
 
     shape = jax.ShapeDtypeStruct
-    tendency, outgoing, gather_sum, send_rows = call(
-        physics_kernel,
+    tendency, outgoing, gather_sum, send_rows, table = call(
+        partial(physics_kernel, per),
         (
             shape((rows, cols), F32),
             shape((devices * per, rows + EXTRA), F32),
             shape((cols, cols), BF16),
             shape((2 * edge, cols), BF16),
+            shape((TABLE_ROWS, cols), F32),
         ),
         (
             pltpu.VMEM((rows, rows), BF16),
             pltpu.VMEM((rows, rows), BF16),
             pltpu.VMEM((rows, rows), F32),
             pltpu.VMEM((rows, cols), F32),
+            pltpu.VMEM((levels, rows), F32),
         ),
-        smem=1,
-        inputs=5,
-    )(trips, table, flat, mix, coupling)
+        inputs=7,
+    )(flat, metric, neighbours, cost_class, slots, level_mix, field_coupling_matrix)
     out, physics = call(
         partial(exchange_kernel, levels, per),
         (shape((rows, cols), F32), shape((rows, cols), F32)),
@@ -339,10 +378,10 @@
             pltpu.SemaphoreType.DMA((devices,)),
             pltpu.SemaphoreType.DMA((devices,)),
         ),
-        inputs=9,
+        inputs=8,
         collective_id=0,
         has_side_effects=True,
-    )(flat, tendency, weight, dhi, dlo, gather_sum, send_rows, table, outgoing)
+    )(flat, tendency, dhi, dlo, gather_sum, send_rows, table, outgoing)
     return out.reshape(state.shape), physics.reshape(state.shape)
 
 

time: 122 us -> 98.7 us (0.81)
  other arithmetic: 8.64 us -> 0 us
  local copies, waits for them, and re-layouts: 12 us -> 5.32 us
  between operations: 5.88 us -> 0.66 us
  Pallas kernels: 94.5 us -> 92.1 us
    pallas_call x1, Pallas kernels: 79.8 us -> 76.6 us  [per_device(): call(partial(exchange_kernel, levels, per), (shape((rows, cols), F32), sh...]
    add x1 -> x0, other arithmetic: 2.56 us -> none  [index_table(): by_slot = by_slot // pair * per + by_slot % pair]
    reshape x6 -> x0, local copies, waits for them, and re-layouts: 2.48 us -> none  [the longest x1 0.84 us: per_device(): mix = jnp.transpose(level_mix, (1, 0, 2)).reshape(levels, rows)]
    reduce_sum x4 -> x0, other arithmetic: 2.19 us -> none  [the longest x1 1.46 us: index_table(): jnp.sum((classes >= q).astype(jnp.int32))]
    transpose x4 -> x0, local copies, waits for them, and re-layouts: 2.06 us -> none  [the longest x1 1.14 us: per_device(): mix = jnp.transpose(level_mix, (1, 0, 2)).reshape(levels, rows)]
    broadcast_in_dim x11 -> x0, local copies, waits for them, and re-layouts: 1.5 us -> none  [the longest x1 0.77 us: per_device(): jnp.broadcast_to(field_coupling_matrix[:, :, None], (fields, fields, leve...]
    mul x6 -> x0, other arithmetic: 1.44 us -> none  [the longest x1 0.77 us: index_table(): points * north + ix]
    another operation x3 -> x0, local copies, waits for them, and re-layouts: 1.25 us -> none  [index_table(): return (jnp.stack(rows), trips)]
where the time goes in v3:
time: 98.7 us; the launch traced here: 98.1 us
  Pallas kernels  92.1 us (93%)
  local copies, waits for them, and re-layouts  5.32 us (5%)
    pallas_call x1, Pallas kernels, per_device(): call(partial(exchange_kernel, levels, per), (shape((rows, cols), F32), sh...  76.6 us
    pallas_call x1, Pallas kernels, per_device(): call(partial(physics_kernel, per), (shape((rows, cols), F32), shape((devi...  15.5 us
    unnamed x6, local copies, waits for them, and re-layouts  4.65 us

profile of v3, /device:TPU:0, one launch (start us, length us, event | category | flops | bytes accessed | tf_op | source)
XLA Modules:
  0.0 98.1 jit_solution(4091496319986266050)
XLA Ops:
  0.6 0.0 copy-start
  0.7 0.8 copy-done
  1.5 0.7 constant_dynamic-slice_fusion.slots
  2.1 15.5 %shard_map.104 = (f32[720,512]{1,0:T(8,128)}, f32[512,728]{1,0:T(8,128)}, bf16[512,512]{1,0:T(8,128)(2,1)}, bf16[64,512]{1,0:T(8,128)(2,1)}, f32[8,512]{1,0:T(8,128)}) custom-call(f32[720,512]{1,0:T(8,128)} %bitcast.3, f32[16,32]{1,0:T(8,128)} %metric.1, s32[4,32]{1,0:T(4,128)} %neighbours.1, s32[16,32]{1,0:T(8,128)} %classes.1, ...), custom_call_target="tpu_custom_call" | custom-call | tf_op jit(solution)/shard_map/pallas_call | solution.py:351
  17.6 76.6 %shard_map.105 = (f32[720,512]{1,0:T(8,128)}, f32[720,512]{1,0:T(8,128)}) custom-call(f32[720,512]{1,0:T(8,128)} %bitcast.4, f32[720,512]{1,0:T(8,128)} %get-tuple-element.9.tendency, bf16[256,512]{1,0:T(8,128)(2,1)} %constant.21.clone.dhi, bf16[256,512]{1,0:T(8,128)(2,1)} %constant.22.clone.dlo, bf16[512,512]{1,0:T(8,128)(2,1)} %get-tuple-element.10.gather_sum, ...), custom_call_target="tpu_custom_call" | custom-call | tf_op jit(solution)/shard_map/pallas_call | solution.py:369
  94.3 0.0 copy-start.1
  94.3 2.7 %copy.13 = f32[10,72,512]{2,1,0:T(8,128)} copy(f32[10,72,512]{2,1,0:T(8,128)} %bitcast.6) | data formatting | bytes 2949120
  97.0 0.0 copy-done.1
  97.0 1.1 %copy.14 = f32[10,72,512]{2,1,0:T(8,128)} copy(f32[10,72,512]{2,1,0:T(8,128)S(1)} %bitcast.5) | data formatting | bytes 2949120
Async XLA Ops:
  0.6 0.8 copy-start
  94.3 2.7 %copy-start.1 = (f32[720,512]{1,0:T(8,128)S(1)}, f32[720,512]{1,0:T(8,128)}, u32[]{:S(2)}) copy-start(f32[720,512]{1,0:T(8,128)} %get-tuple-element.15) | copy-start | bytes 4423684

commit v4 on v3

--- a/solution.py
+++ b/solution.py
@@ -1,3 +1,4 @@
+import math
 from functools import partial
 
 import jax
@@ -270,8 +271,10 @@
             device_id_type=pl.DeviceIdType.MESH,
         )
 
+    stride = next(n for n in (13, 11, 7, 5, 3, 1) if math.gcd(n, devices) == 1)
+
     def far(i):
-        other, where = device(i)
+        other, where = device(lax.rem(i * stride, devices))
         return pltpu.make_async_remote_copy(
             src_ref=outgoing.at[pl.ds(pl.multiple_of(other * per, 8), per)],
             dst_ref=arrived.at[pl.ds(pl.multiple_of(myself * per, 8), per)],
@@ -294,25 +297,26 @@
             current, tendency[...], table[WEIGHT : WEIGHT + 1, :], dhi[...], dlo[...], gather_sum[...], send_rows[...], levels
         )
 
+    others = devices - 1
+    cuts = [1, 1 + others * 7 // 31, 1 + others * 17 // 31, 1 + others * 27 // 31, devices]
+    pl.semaphore_wait(barrier, others)
+    lax.fori_loop(cuts[0], cuts[1], start_far, 0)
     local, edges = advance(state[...])
     sent[0] = edges
-    pl.semaphore_wait(barrier, devices - 1)
     near(0, 0).start()
     near(0, 1).start()
-    cuts = [1, 1 + (devices - 1) // 4, 1 + (devices - 1) // 2, devices]
-    lax.fori_loop(cuts[0], cuts[1], start_far, 0)
     mine = pl.ds(pl.multiple_of(myself * per, 8), per)
     arrived[mine, :] = outgoing[mine, :]
     for step in range(SUBSTEPS):
         near(step, 0).wait()
         near(step, 1).wait()
+        lax.fori_loop(cuts[step + 1], cuts[step + 2], start_far, 0)
         current = settle(local, received[step, :edge], received[step, edge:], table[...], rows)
         if step < SUBSTEPS - 1:
             local, edges = advance(current)
             sent[step + 1] = edges
             near(step + 1, 0).start()
             near(step + 1, 1).start()
-            lax.fori_loop(cuts[step + 1], cuts[step + 2], start_far, 0)
         else:
             out[...] = current
     lax.fori_loop(1, devices, wait_far, 0)

time: 98.7 us -> 104 us (1.054)
  Pallas kernels: 92.1 us -> 97.3 us
    pallas_call x1, Pallas kernels: 76.6 us -> 81.8 us  [per_device(): call(partial(exchange_kernel, levels, per), (shape((rows, cols), F32), sh...]
where the time goes in v4:
time: 104 us; the launch traced here: 103 us
  Pallas kernels  97.3 us (94%)
  local copies, waits for them, and re-layouts  5.32 us (5%)
    pallas_call x1, Pallas kernels, per_device(): call(partial(exchange_kernel, levels, per), (shape((rows, cols), F32), sh...  81.8 us
    pallas_call x1, Pallas kernels, per_device(): call(partial(physics_kernel, per), (shape((rows, cols), F32), shape((devi...  15.5 us
    unnamed x6, local copies, waits for them, and re-layouts  4.65 us

profile of v4, /device:TPU:0, one launch (start us, length us, event | category | flops | bytes accessed | tf_op | source)
XLA Modules:
  0.0 103.3 jit_solution(15423200806660903356)
XLA Ops:
  0.6 0.0 copy-start
  0.7 0.8 copy-done
  1.5 0.7 constant_dynamic-slice_fusion.slots
  2.1 15.5 %shard_map.104 = (f32[720,512]{1,0:T(8,128)}, f32[512,728]{1,0:T(8,128)}, bf16[512,512]{1,0:T(8,128)(2,1)}, bf16[64,512]{1,0:T(8,128)(2,1)}, f32[8,512]{1,0:T(8,128)}) custom-call(f32[720,512]{1,0:T(8,128)} %bitcast.3, f32[16,32]{1,0:T(8,128)} %metric.1, s32[4,32]{1,0:T(4,128)} %neighbours.1, s32[16,32]{1,0:T(8,128)} %classes.1, ...), custom_call_target="tpu_custom_call" | custom-call | tf_op jit(solution)/shard_map/pallas_call | solution.py:355
  17.6 81.8 %shard_map.105 = (f32[720,512]{1,0:T(8,128)}, f32[720,512]{1,0:T(8,128)}) custom-call(f32[720,512]{1,0:T(8,128)} %bitcast.4, f32[720,512]{1,0:T(8,128)} %get-tuple-element.9.tendency, bf16[256,512]{1,0:T(8,128)(2,1)} %constant.21.clone.dhi, bf16[256,512]{1,0:T(8,128)(2,1)} %constant.22.clone.dlo, bf16[512,512]{1,0:T(8,128)(2,1)} %get-tuple-element.10.gather_sum, ...), custom_call_target="tpu_custom_call" | custom-call | tf_op jit(solution)/shard_map/pallas_call | solution.py:373
  99.5 0.0 copy-start.1
  99.5 2.7 %copy.13 = f32[10,72,512]{2,1,0:T(8,128)} copy(f32[10,72,512]{2,1,0:T(8,128)} %bitcast.6) | data formatting | bytes 2949120
  102.2 0.0 copy-done.1
  102.2 1.1 %copy.14 = f32[10,72,512]{2,1,0:T(8,128)} copy(f32[10,72,512]{2,1,0:T(8,128)S(1)} %bitcast.5) | data formatting | bytes 2949120
Async XLA Ops:
  0.6 0.8 copy-start
  99.5 2.7 %copy-start.1 = (f32[720,512]{1,0:T(8,128)S(1)}, f32[720,512]{1,0:T(8,128)}, u32[]{:S(2)}) copy-start(f32[720,512]{1,0:T(8,128)} %get-tuple-element.15) | copy-start | bytes 4423684

commit v5 on v4

--- a/solution.py
+++ b/solution.py
@@ -1,4 +1,3 @@
-import math
 from functools import partial
 
 import jax
@@ -271,10 +270,8 @@
             device_id_type=pl.DeviceIdType.MESH,
         )
 
-    stride = next(n for n in (13, 11, 7, 5, 3, 1) if math.gcd(n, devices) == 1)
-
     def far(i):
-        other, where = device(lax.rem(i * stride, devices))
+        other, where = device(i)
         return pltpu.make_async_remote_copy(
             src_ref=outgoing.at[pl.ds(pl.multiple_of(other * per, 8), per)],
             dst_ref=arrived.at[pl.ds(pl.multiple_of(myself * per, 8), per)],
@@ -298,7 +295,7 @@
         )
 
     others = devices - 1
-    cuts = [1, 1 + others * 7 // 31, 1 + others * 17 // 31, 1 + others * 27 // 31, devices]
+    cuts = [1, 1 + others * 6 // 31, 1 + others * 14 // 31, 1 + others * 22 // 31, devices]
     pl.semaphore_wait(barrier, others)
     lax.fori_loop(cuts[0], cuts[1], start_far, 0)
     local, edges = advance(state[...])

time: 104 us -> 101 us (0.971)
  Pallas kernels: 97.3 us -> 93.4 us
    pallas_call x1, Pallas kernels: 81.8 us -> 78 us  [per_device(): call(partial(exchange_kernel, levels, per), (shape((rows, cols), F32), sh...]
where the time goes in v5:
time: 101 us; the launch traced here: 99.4 us
  Pallas kernels  93.4 us (92%)
  local copies, waits for them, and re-layouts  5.32 us (5%)
    pallas_call x1, Pallas kernels, per_device(): call(partial(exchange_kernel, levels, per), (shape((rows, cols), F32), sh...  78 us
    pallas_call x1, Pallas kernels, per_device(): call(partial(physics_kernel, per), (shape((rows, cols), F32), shape((devi...  15.5 us
    unnamed x6, local copies, waits for them, and re-layouts  4.65 us

profile of v5, /device:TPU:0, one launch (start us, length us, event | category | flops | bytes accessed | tf_op | source)
XLA Modules:
  0.0 99.4 jit_solution(9896134284450882642)
XLA Ops:
  0.6 0.0 copy-start
  0.7 0.8 copy-done
  1.5 0.7 constant_dynamic-slice_fusion.slots
  2.1 15.5 %shard_map.104 = (f32[720,512]{1,0:T(8,128)}, f32[512,728]{1,0:T(8,128)}, bf16[512,512]{1,0:T(8,128)(2,1)}, bf16[64,512]{1,0:T(8,128)(2,1)}, f32[8,512]{1,0:T(8,128)}) custom-call(f32[720,512]{1,0:T(8,128)} %bitcast.3, f32[16,32]{1,0:T(8,128)} %metric.1, s32[4,32]{1,0:T(4,128)} %neighbours.1, s32[16,32]{1,0:T(8,128)} %classes.1, ...), custom_call_target="tpu_custom_call" | custom-call | tf_op jit(solution)/shard_map/pallas_call | solution.py:352
  17.6 78.0 %shard_map.105 = (f32[720,512]{1,0:T(8,128)}, f32[720,512]{1,0:T(8,128)}) custom-call(f32[720,512]{1,0:T(8,128)} %bitcast.4, f32[720,512]{1,0:T(8,128)} %get-tuple-element.9.tendency, bf16[256,512]{1,0:T(8,128)(2,1)} %constant.21.clone.dhi, bf16[256,512]{1,0:T(8,128)(2,1)} %constant.22.clone.dlo, bf16[512,512]{1,0:T(8,128)(2,1)} %get-tuple-element.10.gather_sum, ...), custom_call_target="tpu_custom_call" | custom-call | tf_op jit(solution)/shard_map/pallas_call | solution.py:370
  95.6 0.0 copy-start.1
  95.6 2.7 %copy.13 = f32[10,72,512]{2,1,0:T(8,128)} copy(f32[10,72,512]{2,1,0:T(8,128)} %bitcast.6) | data formatting | bytes 2949120
  98.3 0.0 copy-done.1
  98.3 1.1 %copy.14 = f32[10,72,512]{2,1,0:T(8,128)} copy(f32[10,72,512]{2,1,0:T(8,128)S(1)} %bitcast.5) | data formatting | bytes 2949120
Async XLA Ops:
  0.6 0.8 copy-start
  95.6 2.7 %copy-start.1 = (f32[720,512]{1,0:T(8,128)S(1)}, f32[720,512]{1,0:T(8,128)}, u32[]{:S(2)}) copy-start(f32[720,512]{1,0:T(8,128)} %get-tuple-element.15) | copy-start | bytes 4423684
